TPU v7x, 128 devices: a whole 4x4x4 slice. The times are simulated.
128 devices in a mesh: grp: 8 (over z, core), seq: 16 (over x, y).
Axes of the slice: x: 4, y: 4, z: 4, core: 2. Of those that a mesh axis runs over, the one named last changes fastest.
Arguments:
- prefill_kv: bfloat16 [32, 2048, 2048], P(None, ('grp', 'seq')), may hold values from -6 to 6
- prefill_vscale: bfloat16 [32, 2048], P(None, ('grp', 'seq')), may hold values from 0.29882812 to 3
- k_scale: float32 [32, 1024], replicated, may hold values from 0.5 to 6
- resident_kv: bfloat16 [32, 4096, 2048], P('grp', 'seq'), may hold values from -6 to 6
- resident_vscale: bfloat16 [32, 4096], P('grp', 'seq'), may hold values from 0.29882812 to 3
- queries: bfloat16 [32, 4, 16384], P('grp'), may hold values from -6 to 6
- route: int32 [32], replicated, may hold values from 0 to 31, each once
- lengths: int32 [32], replicated, may hold values from 1 to 2048, 32768 in all
Outputs:
- attn_out: bfloat16 [32, 4, 16384], P('grp', None, 'seq')
- decode_cache: bfloat16 [16, 32, 128, 2048], P('seq', 'grp')
- decode_vscale: bfloat16 [16, 32, 128], P('seq', 'grp')
Inputs may be any that keep to these rules, and one draw needn't show every extreme that they name: `route`: each request is served by exactly one slot; slot j belongs to decode group j // 4. Live prefill positions are 0 to lengths - 1; some request has exactly 2048.
All inputs are finite; a program needn't handle non-finite values.
Results may differ from a plain program's by a relative error of at most 0.0081.
Values may be sent and summed in bfloat16 or wider, within the bound.
No kernel may reach another device: no remote copies, remote signals or barrier semaphores. Data moves between devices by JAX's collectives and lax.ppermute only.
A program may use at most 64 MiB of HBM per device.

v0:
```python
import jax
import jax.numpy as jnp
from jax import lax
from jax.sharding import PartitionSpec as P

HEAD_DIM = 128


def body(
    prefill_kv, prefill_vscale, k_scale, resident_kv, resident_vscale, queries, route, lengths
):
    groups = lax.axis_size("grp")
    splits = lax.axis_size("seq")
    group_index = lax.axis_index("grp")
    split_index = lax.axis_index("seq")
    requests, shard_len, row_width = prefill_kv.shape
    per_group = requests // groups
    sub_len = shard_len // splits
    key_width = row_width // 2
    kv_heads = key_width // HEAD_DIM
    head_count = queries.shape[2] // HEAD_DIM
    group_heads = head_count // kv_heads
    steps_count = queries.shape[1]
    send_index = (
        route.reshape(groups, per_group).T[:, :, None] * splits
        + lax.iota(jnp.int32, splits)[None, None, :]
    )
    blocks = prefill_kv.reshape(requests * splits, sub_len, row_width)
    scale_blocks = prefill_vscale.reshape(requests * splits, sub_len)
    outgoing = jnp.take(blocks, send_index, axis=0)
    out_scales = jnp.take(scale_blocks, send_index, axis=0)
    arrived, arrived_scale = (
        lax.all_to_all(
            outgoing.reshape(per_group, groups * splits * sub_len, row_width),
            ("grp", "seq"),
            split_axis=1,
            concat_axis=1,
            tiled=True,
        ),
        lax.all_to_all(
            out_scales.reshape(per_group, groups * splits * sub_len),
            ("grp", "seq"),
            split_axis=1,
            concat_axis=1,
            tiled=True,
        ),
    )
    my_requests = lax.dynamic_slice_in_dim(route, group_index * per_group, per_group)
    choose = my_requests[:, None] == lax.iota(jnp.int32, requests)[None, :]
    key_scale = jnp.dot(choose.astype(jnp.float32), k_scale, precision=lax.Precision.HIGHEST)
    live_len = jnp.sum(jnp.where(choose, lengths[None, :], 0), axis=1)
    query_rows = queries.astype(jnp.float32).reshape(
        per_group, steps_count, kv_heads, group_heads, HEAD_DIM
    )
    scaled = (
        query_rows * key_scale.reshape(per_group, 1, kv_heads, 1, HEAD_DIM) * HEAD_DIM ** (-0.5)
    ).astype(jnp.bfloat16)
    res_keys = resident_kv[:, :, :key_width].reshape(per_group, -1, kv_heads, HEAD_DIM)
    res_vals = resident_kv[:, :, key_width:].reshape(per_group, -1, kv_heads, HEAD_DIM)
    new_keys = arrived[:, :, :key_width].reshape(per_group, -1, kv_heads, HEAD_DIM)
    new_vals = arrived[:, :, key_width:].reshape(per_group, -1, kv_heads, HEAD_DIM)
    res_scores = jnp.einsum(
        "jsngd,jrnd->jsngr", scaled, res_keys, preferred_element_type=jnp.float32
    )
    new_scores = jnp.einsum(
        "jsngd,jknd->jsngk", scaled, new_keys, preferred_element_type=jnp.float32
    )
    moved_len = new_keys.shape[1]
    token_ids = lax.iota(jnp.int32, moved_len)
    positions = token_ids // sub_len * shard_len + split_index * sub_len + token_ids % sub_len
    live_mask = positions[None, :] < live_len[:, None]
    new_scores = jnp.where(live_mask[:, None, None, None, :], new_scores, -jnp.inf)
    local_top = jnp.maximum(jnp.max(res_scores, axis=-1), jnp.max(new_scores, axis=-1))
    row_top = lax.pmax(local_top, "seq")
    res_expo = jnp.exp(res_scores - row_top[..., None])
    new_expo = jnp.exp(new_scores - row_top[..., None])
    partial_total = jnp.sum(res_expo, axis=-1) + jnp.sum(new_expo, axis=-1)
    res_weight = (res_expo * resident_vscale.astype(jnp.float32)[:, None, None, None, :]).astype(
        jnp.bfloat16
    )
    new_weight = (new_expo * arrived_scale.astype(jnp.float32)[:, None, None, None, :]).astype(
        jnp.bfloat16
    )
    numerator = jnp.einsum(
        "jsngr,jrnd->jsngd", res_weight, res_vals, preferred_element_type=jnp.float32
    )
    numerator = numerator + jnp.einsum(
        "jsngk,jknd->jsngd", new_weight, new_vals, preferred_element_type=jnp.float32
    )
    numerator = numerator.reshape(per_group, steps_count, head_count, HEAD_DIM)
    partial_total = partial_total.reshape(per_group, steps_count, head_count)
    head_share = head_count // splits
    summed, denominator = lax.psum((numerator, partial_total), "seq")
    summed = lax.dynamic_slice_in_dim(summed, split_index * head_share, head_share, 2)
    denominator = lax.dynamic_slice_in_dim(denominator, split_index * head_share, head_share, 2)
    attended = (summed / denominator[..., None]).astype(jnp.bfloat16)
    attended = attended.reshape(per_group, steps_count, head_share * HEAD_DIM)
    return (attended, arrived[None], arrived_scale[None])


def solution(mesh):
    in_specs = (
        P(None, ("grp", "seq"), None),
        P(None, ("grp", "seq")),
        P(),
        P("grp", "seq", None),
        P("grp", "seq"),
        P("grp", None, None),
        P(),
        P(),
    )
    out_specs = (P("grp", None, "seq"), P("seq", "grp", None, None), P("seq", "grp", None))
    return jax.shard_map(body, mesh=mesh, in_specs=in_specs, out_specs=out_specs, check_vma=False)
```

profile of v0, /device:TPU:0, one launch (start us, length us, event | category | flops | bytes accessed | tf_op | source)
XLA Modules:
  0.0 249.7 jit_solution(17153594664272911838)
XLA Ops:
  7.2 0.0 copy-start
  7.2 0.8 broadcast_multiply_fusion
  8.0 0.1 mul.72
  8.1 0.1 copy.86
  8.2 0.1 add.140
  8.2 0.8 copy.95
  9.0 0.1 reshape.213
  9.1 0.1 compare_select_fusion
  9.2 0.1 add.137
  9.2 0.1 add.150
  9.3 0.1 reshape.207
  9.4 3.5 %gather_fusion.1 = bf16[512]{0:T(512)(128)(2,1)S(1)} fusion(bf16[512]{0:T(512)(128)(2,1)S(1)} %reshape.213, s32[1024]{0:T(1024)S(1)} %pad_clamp_fusion), kind=kCustom, calls=%fused_computation.1 | custom fusion | bytes 4096 | tf_op jit(solution)/shard_map/jit(_take)/gather | solution.py:31
  13.0 0.8 copy.96
  13.7 11.1 %all-to-all-start.1 = ((bf16[4,128,1]{0,2,1:T(2,128)(2,1)}), bf16[4,128,1]{0,2,1:T(2,128)(2,1)S(1)}, u32[]{:S(2)}, u32[]{:S(2)}) async-start(bf16[4,128,1]{0,2,1:T(2,128)(2,1)} %copy.96), calls=%async_computation.1 | async-start | bytes 131072 | tf_op jit(solution)/shard_map/all_to_all | solution.py:40
  24.9 0.1 add.138
  25.0 0.1 copy.87
  25.1 0.0 copy-done
  25.1 3.3 %gather_fusion = bf16[512,2048]{1,0:T(8,128)(2,1)} fusion(bf16[512,2048]{1,0:T(8,128)(2,1)S(1)} %bitcast.65, s32[1024]{0:T(1024)S(1)} %pad_clamp_fusion), kind=kCustom, calls=%fused_computation | custom fusion | bytes 4196352 | tf_op jit(solution)/shard_map/jit(_take)/gather | solution.py:30
  28.4 4.7 %copy_select_fusion = bf16[4,128,2048]{2,0,1:T(4,128)(2,1)} fusion(bf16[4,128,2048]{2,1,0:T(8,128)(2,1)} %bitcast.68, pred[4,128]{0,1:T(8,128)(4,1)S(1)} %copy.87), kind=kLoop, calls=%fused_computation.5 | loop fusion | flops 1048576 | bytes 4194816 | tf_op jit(solution)/shard_map/jit(_take)/select_n | solution.py:30
  33.1 0.0 copy-start.6
  33.1 0.0 copy-start.4
  33.1 1.2 all-to-all-done.1
  34.3 9.1 %all-to-all-start = ((bf16[4,128,2048]{2,0,1:T(4,128)(2,1)}), bf16[4,128,2048]{2,0,1:T(4,128)(2,1)}, u32[]{:S(2)}, u32[]{:S(2)}) async-start(bf16[4,128,2048]{2,0,1:T(4,128)(2,1)} %copy_select_fusion), calls=%async_computation | async-start | bytes 4194304 | tf_op jit(solution)/shard_map/all_to_all | solution.py:33
  43.4 0.0 all-reduce.2.cloned.1.call-start
  43.5 0.0 copy-done.6
  43.5 0.1 dynamic_slice.9
  43.6 0.0 copy-done.5
  43.6 0.0 copy-done.4
  43.6 0.2 convolution_bitcast_fusion.2
  43.8 1.5 reshape.201
  45.3 0.0 copy-start.3
  45.3 5.0 %fusion.17 = (bf16[4,256,1024]{2,1,0:T(8,128)(2,1)}, bf16[4,256,1024]{2,1,0:T(8,128)(2,1)}) fusion(bf16[4,256,2048]{2,1,0:T(8,128)(2,1)} %param.11), kind=kLoop, calls=%fused_computation.42 | loop fusion | bytes 8388608 | tf_op jit(solution)/shard_map/slice | solution.py:59
  50.3 4.0 %copy.117 = bf16[4,256,1024]{1,2,0:T(8,128)(2,1)} copy(bf16[4,256,1024]{2,1,0:T(8,128)(2,1)} %get-tuple-element.18) | data formatting | bytes 4194304
  54.3 0.0 copy-start.7
  54.3 3.9 %copy.115 = bf16[4,256,1024]{1,2,0:T(8,128)(2,1)} copy(bf16[4,256,1024]{2,1,0:T(8,128)(2,1)} %get-tuple-element.19) | data formatting | bytes 4194304
  58.3 0.0 copy-done.7
  58.3 0.2 select_reduce_fusion
  58.4 0.1 broadcast_compare_fusion
  58.5 0.0 copy-done.3
  58.5 3.4 %bitcast_reduce_fusion = (f32[4,4,8,16]{3,1,2,0:T(4,128)S(1)}, f32[4,8,4,16,256]{4,3,2,1,0:T(8,128)}) fusion(bf16[4,256,8,128,1]{1,3,4,2,0:T(8,128)(2,1)} %bitcast.67, f32[4,4,8,16,128]{4,3,2,1,0:T(8,128)S(1)} %reshape.201, f32[4,8,128]{2,1,0:T(8,128)S(1)} %bitcast.73), kind=kOutput, calls=%fused_computation.3 | convolution fusion | flops 135526400 | bytes 5267456 | tf_op jit(solution)/shard_map/jsngd,jrnd->jsngr/dot_general | solution.py:62
  61.9 0.1 convert_element_type.34
  62.0 0.1 copy.97
  62.1 10.6 %all-to-all-done = bf16[4,128,2048]{2,0,1:T(4,128)(2,1)} async-done(((bf16[4,128,2048]{2,0,1:T(4,128)(2,1)}), bf16[4,128,2048]{2,0,1:T(4,128)(2,1)}, u32[]{:S(2)}, u32[]{:S(2)}) %all-to-all-start) | async-done | bytes 2097184 | tf_op jit(solution)/shard_map/all_to_all | solution.py:33
  72.7 3.2 %fusion.18 = (bf16[4,128,1024]{2,0,1:T(4,128)(2,1)}, bf16[4,128,1024]{2,0,1:T(4,128)(2,1)S(1)}) fusion(bf16[4,128,2048]{2,0,1:T(4,128)(2,1)} %all-to-all-done), kind=kLoop, calls=%fused_computation.43 | loop fusion | bytes 4194304 | tf_op jit(solution)/shard_map/slice | solution.py:60
  75.9 2.7 %copy.116 = bf16[4,128,1024]{1,2,0:T(8,128)(2,1)} copy(bf16[4,128,1024]{2,0,1:T(4,128)(2,1)} %get-tuple-element.20) | data formatting | bytes 2097152
  78.6 1.7 copy.118
  80.3 2.0 fusion.19
  82.4 72.1 %pmax.7 = f32[4,4,8,16]{3,1,2,0:T(4,128)S(1)} all-reduce(f32[4,4,8,16]{3,1,2,0:T(4,128)S(1)} %max.5), channel_id=1, replica_groups=mesh['grp'=8,'seq'=16] {'seq'}, use_global_device_ids=true, to_apply=%region_3.4 | all-reduce | flops 2048 | bytes 16384 | tf_op jit(solution)/shard_map/pmax | solution.py:74
  154.4 2.2 convolution_bitcast_fusion.1
  156.7 0.0 copy-done.1
  156.7 2.5 %fusion.2 = f32[4,4,8,16,128]{4,3,1,2,0:T(8,128)S(1)} fusion(f32[4,4,8,16,128]{4,3,1,2,0:T(8,128)S(1)} %convolution_bitcast_fusion.1, bf16[4,256,8,128,1]{1,3,4,2,0:T(8,128)(2,1)} %bitcast.66, f32[4,8,4,16,256]{4,3,2,1,0:T(8,128)S(1)} %copy-done.1, f32[4,256]{1,0:T(4,128)S(1)} %convert_element_type.28, f32[4,4,8,16]{3,1,2,0:T(4,128)S(1)} %pmax.7), kind=kOutput, calls=%fused_computation.9 | convolution fusion | flops 136052736 | bytes 6303744 | tf_op jit(solution)/shard_map/jsngr,jrnd->jsngd/dot_general | solution.py:84
  159.2 1.1 copy.99
  160.3 0.0 all-reduce.2.cloned.1.call-update
  160.3 0.7 copy.101
  161.0 4.3 %copy.102 = bf16[1,4,128,2048]{3,2,1,0:T(8,128)(2,1)} copy(bf16[1,4,128,2048]{3,1,2,0:T(4,128)(2,1)} %bitcast.18) | data formatting | bytes 4194304
  165.3 0.7 fusion.8
  166.0 0.0 copy-done.2
  166.0 0.7 fusion.1
  166.8 0.1 add.158
  166.9 36.0 %psum.15 = f32[4,4,128]{2,1,0:T(4,128)S(1)} all-reduce(f32[4,4,128]{2,1,0:T(4,128)S(1)} %add.158), channel_id=1, replica_groups=mesh['grp'=8,'seq'=16] {'seq'}, use_global_device_ids=true, to_apply=%region_7.8 | all-reduce | flops 2048 | bytes 16384 | tf_op jit(solution)/shard_map/psum | solution.py:93
  202.9 0.1 constant_dynamic-slice_fusion
  203.0 38.3 %all-reduce.2.cloned.1.call-done = f32[4,4,128,128]{3,2,1,0:T(8,128)} async-done(((f32[4,4,128,128]{3,2,1,0:T(8,128)}), f32[4,4,128,128]{3,2,1,0:T(8,128)}) %all-reduce.2.cloned.1.call-update) | async-done | bytes 1048592 | tf_op jit(solution)/shard_map/psum | solution.py:93
  241.3 0.9 divide_convert_fusion
  242.2 0.6 reshape.199
  (13 shorter events, 0.1 us)
Async XLA Ops:
  7.2 17.9 %copy-start = (bf16[32,16,2048]{2,1,0:T(8,128)(2,1)S(1)}, bf16[32,16,2048]{2,1,0:T(8,128)(2,1)}, u32[]{:S(2)}) copy-start(bf16[32,16,2048]{2,1,0:T(8,128)(2,1)} %param.8) | copy-start | bytes 6291460
  13.7 20.6 %all-to-all-start.1 = ((bf16[4,128,1]{0,2,1:T(2,128)(2,1)}), bf16[4,128,1]{0,2,1:T(2,128)(2,1)S(1)}, u32[]{:S(2)}, u32[]{:S(2)}) async-start(bf16[4,128,1]{0,2,1:T(2,128)(2,1)} %copy.96), calls=%async_computation.1 | async-start | bytes 131072 | tf_op jit(solution)/shard_map/all_to_all | solution.py:40
  33.1 10.4 %copy-start.6 = (s32[32]{0:T(128)S(1)}, s32[32]{0:T(128)}, u32[]{:S(2)}) copy-start(s32[32]{0:T(128)} %param.14) | copy-start | bytes 388
  33.1 10.5 %copy-start.5 = (bf16[4,256]{1,0:T(4,128)(2,1)S(1)}, bf16[4,256]{1,0:T(4,128)(2,1)}, u32[]{:S(2)}) copy-start(bf16[4,256]{1,0:T(4,128)(2,1)} %param.12) | copy-start | bytes 6148
  33.1 10.5 %copy-start.4 = (f32[32,1024]{1,0:T(8,128)S(1)}, f32[32,1024]{1,0:T(8,128)}, u32[]{:S(2)}) copy-start(f32[32,1024]{1,0:T(8,128)} %param.10) | copy-start | bytes 393220
  34.3 38.4 %all-to-all-start = ((bf16[4,128,2048]{2,0,1:T(4,128)(2,1)}), bf16[4,128,2048]{2,0,1:T(4,128)(2,1)}, u32[]{:S(2)}, u32[]{:S(2)}) async-start(bf16[4,128,2048]{2,0,1:T(4,128)(2,1)} %copy_select_fusion), calls=%async_computation | async-start | bytes 4194304 | tf_op jit(solution)/shard_map/all_to_all | solution.py:33
  43.4 197.9 %all-reduce.2.cloned.1.call-start = ((), (), s32[]{:S(2)}) async-start(), calls=%async_computation.2 | async-start | bytes 2097152 | tf_op jit(solution)/shard_map/psum | solution.py:93
  45.3 13.2 %copy-start.3 = (f32[4,4,8,16,128]{4,3,2,1,0:T(8,128)}, f32[4,4,8,16,128]{4,3,2,1,0:T(8,128)S(1)}, u32[]{:S(2)}) copy-start(f32[4,4,8,16,128]{4,3,2,1,0:T(8,128)S(1)} %reshape.201) | copy-start | bytes 3145732
  54.3 4.0 %copy-start.7 = (s32[32]{0:T(128)S(1)}, s32[32]{0:T(128)}, u32[]{:S(2)}) copy-start(s32[32]{0:T(128)} %param.15) | copy-start | bytes 388
  154.4 2.2 copy-start.1
  161.0 5.1 %copy-start.2 = (f32[4,8,4,16,256]{4,3,2,1,0:T(8,128)S(1)}, f32[4,8,4,16,256]{4,3,2,1,0:T(8,128)}, u32[]{:S(2)}) copy-start(f32[4,8,4,16,256]{4,3,2,1,0:T(8,128)} %get-tuple-element.23) | copy-start | bytes 6291460
Sparse Core Ops, SparseCore 0:
  160.4 80.7 all-reduce.1
where the time goes:
time: 250 us
  blocking collectives  108 us (43%)
  waiting for transfers between devices  50.2 us (20%)
  local copies, waits for them, and re-layouts  38.2 us (15%)
  starting transfers between devices  20.3 us (8%)
  between operations  14.2 us (6%)
  matrix products  10.4 us (4%)
  other arithmetic  8.36 us (3%)
    pmax x1, blocking collectives, body(): row_top = lax.pmax(local_top, 'seq')  72.1 us
    psum x1, waiting for transfers between devices, body(): summed, denominator = lax.psum((numerator, partial_total), 'seq')  38.3 us
    psum x1, blocking collectives, body(): summed, denominator = lax.psum((numerator, partial_total), 'seq')  36 us
    unnamed x23, local copies, waits for them, and re-layouts  17.4 us
    all_to_all x1, starting transfers between devices, body(): lax.all_to_all(out_scales.reshape(per_group, groups * splits * sub_len),...  11.1 us
    all_to_all x1, waiting for transfers between devices, body(): lax.all_to_all(outgoing.reshape(per_group, groups * splits * sub_len, row...  10.6 us
    all_to_all x1, starting transfers between devices, body(): lax.all_to_all(outgoing.reshape(per_group, groups * splits * sub_len, row...  9.07 us
    slice x1, local copies, waits for them, and re-layouts, body(): resident_kv[:, :, key_width:].reshape(per_group, -1, kv_heads, HEAD_DIM)  5.03 us
  transfers between devices with their start and end apart: 3, of which 3 were waited for; matrix products, arithmetic and copies ran while one was open for 13% of the time, Pallas kernels for 0%

commit v1 on v0

v1 whole, which is shorter than its diff:
```python
import jax
import jax.numpy as jnp
from jax import lax
from jax.experimental import pallas as pl
from jax.experimental.pallas import tpu as pltpu
from jax.sharding import PartitionSpec as P

HEAD_DIM = 128
LANES = 128
DEAD = -1e30
MIB = 1 << 20


def swap_matrix():
    row = lax.broadcasted_iota(jnp.int32, (256, 256), 0)
    col = lax.broadcasted_iota(jnp.int32, (256, 256), 1)
    hit = (row // 16 == col % 16) & (row % 16 == col // 16)
    return jnp.where(hit, 1.0, 0.0).astype(jnp.bfloat16)


def pack_kernel(route, kv, vscale, out, scale_out, flat):
    swap = swap_matrix()
    groups = out.shape[0] // 16

    def one_group(g, carry):
        requests = [route[g * 4 + i] for i in range(4)]
        for pair in range(2):
            tiles = []
            for l4 in range(4):
                for i in range(4):
                    halves = [
                        kv[requests[i], :, pl.ds((lg * 4 + l4) * LANES, LANES)]
                        for lg in (2 * pair, 2 * pair + 1)
                    ]
                    tiles.append(jnp.concatenate(halves, axis=1))
            moved = jnp.dot(
                swap, jnp.concatenate(tiles, axis=0), preferred_element_type=jnp.float32
            ).astype(jnp.bfloat16)
            for half in range(2):
                block = moved[:, half * LANES : (half + 1) * LANES].reshape(16, 16, LANES)
                out[pl.ds(g * 16, 16), pl.ds((2 * pair + half) * 16, 16), :] = block
        return carry

    lax.fori_loop(0, groups, one_group, 0)
    flat[...] = jnp.zeros_like(flat)
    flat[0:32, 0:16] = vscale[...].astype(jnp.float32)
    rows = flat[...].T[0:16]
    for g in range(groups):
        for s in range(16):
            scale_out[g * 16 + s] = rows[s : s + 1]


def resident_kernel(route, k_scale, queries, kv, vscale, scaled, numer, top, total, head_scale):
    group = lax.axis_index("grp")
    out_row = lax.broadcasted_iota(jnp.int32, (256, 256), 0)
    in_row = lax.broadcasted_iota(jnp.int32, (256, 256), 1)
    head = (out_row // 32 % 2) * 8 + out_row % 8
    slot_step = out_row // 64 * 4 + out_row // 8 % 4
    hit = (in_row // 16 == head) & (in_row % 16 == slot_step)
    order = jnp.where(hit, 1.0, 0.0).astype(jnp.bfloat16)
    for j in range(4):
        row = k_scale[pl.ds(route[group * 4 + j], 1), :]
        for n in range(8):
            head_scale[j * 8 + n : j * 8 + n + 1, :] = row[:, n * LANES : (n + 1) * LANES]

    def one_head(n, carry):
        tiles = [
            queries[:, pl.ds(pl.multiple_of((n * 16 + h) * LANES, LANES), LANES)] for h in range(16)
        ]
        ordered = jnp.dot(order, jnp.concatenate(tiles, axis=0), preferred_element_type=jnp.float32)
        lanes = pl.ds(pl.multiple_of(n * LANES, LANES), LANES)
        value_lanes = pl.ds(pl.multiple_of((n + 8) * LANES, LANES), LANES)
        for j in range(4):
            key_scale = head_scale[pl.ds(j * 8 + n, 1), :]
            rows = (ordered[j * 64 : (j + 1) * 64] * key_scale * HEAD_DIM ** (-0.5)).astype(jnp.bfloat16)
            scaled[j, n] = rows
            scores = lax.dot_general(
                rows, kv[j, :, lanes], (((1,), (1,)), ((), ())), preferred_element_type=jnp.float32
            )
            high = jnp.max(scores, axis=1, keepdims=True)
            expo = jnp.exp(scores - high)
            weight = (expo * vscale[j : j + 1, :].astype(jnp.float32)).astype(jnp.bfloat16)
            numer[j, n] = jnp.dot(weight, kv[j, :, value_lanes], preferred_element_type=jnp.float32)
            top[j, n] = jnp.broadcast_to(high, (64, LANES))
            total[j, n] = jnp.broadcast_to(jnp.sum(expo, axis=1, keepdims=True), (64, LANES))
        return carry

    lax.fori_loop(0, 8, one_head, 0)


def arrived_kernel(
    route, lengths, arrived, arrived_scale, scaled, numer, top, total,
    cache, cache_scale, partial, stats,
):
    group = lax.axis_index("grp")
    split = lax.axis_index("seq")
    swap = swap_matrix()

    def one_block(b, carry):
        tokens = pl.ds(b * 16, 16)
        for pair in range(2):
            halves = [
                arrived[tokens, pl.ds(lg * 16, 16), :].reshape(256, LANES)
                for lg in (2 * pair, 2 * pair + 1)
            ]
            moved = jnp.dot(
                swap, jnp.concatenate(halves, axis=1), preferred_element_type=jnp.float32
            ).astype(jnp.bfloat16)
            for half in range(2):
                for l4 in range(4):
                    for i in range(4):
                        tile = moved[(l4 * 4 + i) * 16 : (l4 * 4 + i + 1) * 16, half * LANES : (half + 1) * LANES]
                        chunk = (2 * pair + half) * 4 + l4
                        cache[i, tokens, chunk * LANES : (chunk + 1) * LANES] = tile
        return carry

    lax.fori_loop(0, 8, one_block, 0)
    by_request = arrived_scale[...].reshape(LANES, LANES).T
    stats[...] = by_request
    scale_rows = [stats[pl.ds(route[group * 4 + j], 1), :] for j in range(4)]
    for j in range(4):
        cache_scale[j : j + 1, :] = scale_rows[j].astype(jnp.bfloat16)
    positions = lax.broadcasted_iota(jnp.int32, (1, LANES), 1) * 16 + split
    live = [positions < lengths[route[group * 4 + j]] for j in range(4)]
    lane = lax.broadcasted_iota(jnp.int32, (32, LANES), 1)
    stats[...] = jnp.zeros_like(stats)

    def one_head(n, carry):
        lanes = pl.ds(pl.multiple_of(n * LANES, LANES), LANES)
        value_lanes = pl.ds(pl.multiple_of((n + 8) * LANES, LANES), LANES)
        for j in range(4):
            scores = lax.dot_general(
                scaled[j, n], cache[j, :, lanes], (((1,), (1,)), ((), ())),
                preferred_element_type=jnp.float32,
            )
            scores = jnp.where(live[j], scores, DEAD)
            before = top[j, n]
            high = jnp.maximum(before, jnp.max(scores, axis=1, keepdims=True))
            high = high.astype(jnp.bfloat16).astype(jnp.float32)
            expo = jnp.exp(scores - high)
            keep = jnp.exp(before - high)
            weight = (expo * scale_rows[j]).astype(jnp.bfloat16)
            mixed = jnp.dot(weight, cache[j, :, value_lanes], preferred_element_type=jnp.float32)
            mixed = mixed + keep * numer[j, n]
            count = jnp.sum(expo, axis=1, keepdims=True) + keep * total[j, n]
            coarse = count.astype(jnp.bfloat16).astype(jnp.float32)
            for half in range(2):
                part = slice(half * 32, (half + 1) * 32)
                place = n * 2 + half
                partial[place, j * 32 : (j + 1) * 32, :] = mixed[part].astype(jnp.bfloat16)
                at = place * 8
                line = stats[j * 32 : (j + 1) * 32, :]
                line = jnp.where(lane == at, high[part], line)
                line = jnp.where(lane == at + 1, coarse[part], line)
                line = jnp.where(lane == at + 2, (count - coarse)[part], line)
                stats[j * 32 : (j + 1) * 32, :] = line
        return carry

    lax.fori_loop(0, 8, one_head, 0)
    by_place = stats[...].T.reshape(16, 8, LANES)
    by_place = jnp.concatenate([by_place, jnp.zeros_like(by_place)], axis=1)
    partial[:, 128:144, :] = by_place.astype(jnp.bfloat16)


def merge_kernel(partial, out, summed):
    splits = partial.shape[0]
    stat = partial[:, 128:144, :].astype(jnp.float32)
    high = stat[:, 0, :]
    count = stat[:, 1, :] + stat[:, 2, :]
    share = jnp.exp(high - jnp.max(high, axis=0, keepdims=True))
    share = share / jnp.sum(share * count, axis=0, keepdims=True)
    share = jnp.concatenate([share, jnp.zeros((LANES - splits, LANES), jnp.float32)], axis=0).T
    acc = partial[0, 0:128, :].astype(jnp.float32) * share[:, 0:1]
    for s in range(1, splits):
        acc = acc + partial[s, 0:128, :].astype(jnp.float32) * share[:, s : s + 1]
    summed[...] = acc
    for j in range(4):
        for h in range(8):
            out[j, :, h * HEAD_DIM : (h + 1) * HEAD_DIM] = summed[
                pl.ds(j * 32 + h, 4, stride=8), :
            ].astype(jnp.bfloat16)


def call(kernel, outs, args, scalars, scratch=(), limit=32 * MIB, flops=0, name=None):
    smem = pl.BlockSpec(memory_space=pltpu.SMEM)
    vmem = pl.BlockSpec(memory_space=pltpu.VMEM)
    moved = sum(a.size * a.dtype.itemsize for a in list(args) + list(outs))
    return pl.pallas_call(
        kernel,
        out_shape=outs,
        in_specs=[smem] * scalars + [vmem] * (len(args) - scalars),
        out_specs=[vmem] * len(outs),
        scratch_shapes=list(scratch),
        compiler_params=pltpu.CompilerParams(vmem_limit_bytes=limit),
        cost_estimate=pl.CostEstimate(flops=flops, bytes_accessed=moved, transcendentals=0),
        name=name,
    )(*args)


def body(
    prefill_kv, prefill_vscale, k_scale, resident_kv, resident_vscale, queries, route, lengths
):
    shape = jax.ShapeDtypeStruct
    bf16, f32 = jnp.bfloat16, jnp.float32
    square = pltpu.VMEM((LANES, LANES), f32)
    outgoing, out_scales = call(
        pack_kernel,
        [shape((128, 64, LANES), bf16), shape((128, 1, LANES), f32)],
        (route, prefill_kv, prefill_vscale),
        1,
        [square],
        flops=2 * 256 * 256 * 4096,
        name="pack",
    )
    arrived = lax.all_to_all(outgoing, ("grp", "seq"), split_axis=0, concat_axis=0, tiled=True)
    arrived_scale = lax.all_to_all(
        out_scales, ("grp", "seq"), split_axis=0, concat_axis=0, tiled=True
    )
    rows = (4, 8, 64, LANES)
    scaled, numer, top, total = call(
        resident_kernel,
        [shape(rows, bf16), shape(rows, f32), shape(rows, f32), shape(rows, f32)],
        (route, k_scale, queries.reshape(16, -1), resident_kv, resident_vscale),
        1,
        [pltpu.VMEM((32, LANES), f32)],
        flops=4 * 2048 * 256 * 128,
        name="resident",
    )
    cache, cache_scale, partial = call(
        arrived_kernel,
        [shape((4, 128, 2048), bf16), shape((4, 128), bf16), shape((16, 144, LANES), bf16)],
        (route, lengths, arrived, arrived_scale, scaled, numer, top, total),
        2,
        [square],
        flops=4 * 2048 * 128 * 128,
        name="arrived",
    )
    swapped = lax.all_to_all(partial, "seq", split_axis=0, concat_axis=0, tiled=True)
    (attended,) = call(
        merge_kernel,
        [shape((4, 4, 1024), bf16)],
        (swapped,),
        0,
        [square],
        flops=16 * 2 * 128 * 128,
        name="merge",
    )
    return (attended, cache[None], cache_scale[None])


def solution(mesh):
    in_specs = (
        P(None, ("grp", "seq"), None),
        P(None, ("grp", "seq")),
        P(),
        P("grp", "seq", None),
        P("grp", "seq"),
        P("grp", None, None),
        P(),
        P(),
    )
    out_specs = (P("grp", None, "seq"), P("seq", "grp", None, None), P("seq", "grp", None))
    return jax.shard_map(body, mesh=mesh, in_specs=in_specs, out_specs=out_specs, check_vma=False)
```

time: 250 us -> 94.8 us (0.38)
  blocking collectives: 108 us -> 35.9 us
  waiting for transfers between devices: 50.2 us -> 16 us
  local copies, waits for them, and re-layouts: 38.2 us -> 13.2 us
  Pallas kernels: 0 us -> 23.7 us
  starting transfers between devices: 20.3 us -> 4.8 us
  between operations: 14.2 us -> 0.73 us
  matrix products: 10.4 us -> 0 us
  other arithmetic: 8.36 us -> 0 us
    pmax x1 -> x0, blocking collectives: 72.1 us -> none  [body(): row_top = lax.pmax(local_top, 'seq')]
    psum x1 -> x0, waiting for transfers between devices: 38.3 us -> none  [body(): summed, denominator = lax.psum((numerator, partial_total), 'seq')]
    psum x1 -> x0, blocking collectives: 36 us -> none  [body(): summed, denominator = lax.psum((numerator, partial_total), 'seq')]
    all_to_all x0 -> x2, blocking collectives: none -> 35.9 us  [the longest x1 20.4 us: body(): lax.all_to_all(out_scales, ('grp', 'seq'), split_axis=0, concat_axis=0, t...]
    pallas_call x0 -> x4, Pallas kernels: none -> 23.7 us  [call(): pl.pallas_call(kernel, out_shape=outs, in_specs=[smem] * scalars + [vmem]...]
    all_to_all x2 -> x1, starting transfers between devices: 20.2 us -> 4.8 us  [body(): lax.all_to_all(outgoing, ('grp', 'seq'), split_axis=0, concat_axis=0, til...]
    dot_general x5 -> x0, matrix products: 10.4 us -> none  [the longest x1 3.4 us: body(): jnp.einsum('jsngd,jrnd->jsngr', scaled, res_keys, preferred_element_type=...]
    slice x2 -> x0, local copies, waits for them, and re-layouts: 8.26 us -> none  [the longest x1 5.03 us: body(): resident_kv[:, :, key_width:].reshape(per_group, -1, kv_heads, HEAD_DIM)]
  transfers between devices with their start and end apart: 3 -> 1, of which waited for: 3 -> 1; matrix products, arithmetic and copies ran while one was open for 13% -> 0% of each run, Pallas kernels for 0% -> 9%
where the time goes in v1:
time: 94.8 us; the launch traced here: 94.4 us
  blocking collectives  35.9 us (38%)
  Pallas kernels  23.7 us (25%)
  waiting for transfers between devices  16 us (17%)
  local copies, waits for them, and re-layouts  13.2 us (14%)
  starting transfers between devices  4.8 us (5%)
    pallas_call x4, Pallas kernels, call(): pl.pallas_call(kernel, out_shape=outs, in_specs=[smem] * scalars + [vmem]...  23.7 us
    all_to_all x1, blocking collectives, body(): lax.all_to_all(out_scales, ('grp', 'seq'), split_axis=0, concat_axis=0, t...  20.4 us
    all_to_all x1, waiting for transfers between devices, body(): lax.all_to_all(outgoing, ('grp', 'seq'), split_axis=0, concat_axis=0, til...  16 us
    all_to_all x1, blocking collectives, body(): lax.all_to_all(partial, 'seq', split_axis=0, concat_axis=0, tiled=True)  15.5 us
    unnamed x31, local copies, waits for them, and re-layouts  13.1 us
    all_to_all x1, starting transfers between devices, body(): lax.all_to_all(outgoing, ('grp', 'seq'), split_axis=0, concat_axis=0, til...  4.8 us
  transfers between devices with their start and end apart: 1, of which 1 were waited for; matrix products, arithmetic and copies ran while one was open for 0% of the time, Pallas kernels for 9%

profile of v1, /device:TPU:0, one launch (start us, length us, event | category | flops | bytes accessed | tf_op | source)
XLA Modules:
  0.0 94.4 jit_solution(9342889767322091063)
XLA Ops:
  0.6 0.8 copy.11.vscale
  1.4 0.0 copy-start.1
  1.4 1.6 %copy-done.1 = bf16[32,16,2048]{2,1,0:T(8,128)(2,1)S(1)} copy-done((bf16[32,16,2048]{2,1,0:T(8,128)(2,1)S(1)}, bf16[32,16,2048]{2,1,0:T(8,128)(2,1)}, u32[]{:S(2)}) %copy-start.1) | copy-done | bytes 2097176
  3.0 0.0 copy-start.10
  3.0 0.7 copy-done.10
  3.6 2.6 %pack.1 = (bf16[128,64,128]{2,1,0:T(8,128)(2,1)S(1)}, f32[128,1,128]{2,1,0:T(1,128)S(1)}) custom-call(s32[32]{0:T(128)S(1)} %copy-done.10, bf16[32,16,2048]{2,1,0:T(8,128)(2,1)S(1)} %copy-done.1, bf16[32,16]{1,0:T(8,128)(2,1)S(1)} %copy.11.vscale), custom_call_target="tpu_custom_call" | custom-call | flops 536870912 | bytes 4260992 | tf_op jit(solution)/shard_map/pack/pallas_call | solution.py:188
  6.2 0.0 copy-start.2
  6.2 1.3 %copy-done.2 = bf16[128,64,128]{2,1,0:T(8,128)(2,1)} copy-done((bf16[128,64,128]{2,1,0:T(8,128)(2,1)}, bf16[128,64,128]{2,1,0:T(8,128)(2,1)S(1)}, u32[]{:S(2)}) %copy-start.2) | copy-done | bytes 2097176
  7.5 20.4 %all_to_all.15.arrived_scale = f32[128,1,128]{2,1,0:T(1,128)S(1)} all-to-all(f32[128,1,128]{2,1,0:T(1,128)S(1)} %get-tuple-element.13), channel_id=1, replica_groups=mesh['grp'=8,'seq'=16] {'grp','seq'}, dimensions={0} | all-to-all | bytes 131072 | tf_op jit(solution)/shard_map/all_to_all | solution.py:216
  28.0 0.0 copy-start.14
  28.0 0.0 copy-start.9
  28.0 0.0 copy-start.11
  28.0 0.0 copy-start.12
  28.0 4.8 %all-to-all-start = ((bf16[128,64,128]{2,1,0:T(8,128)(2,1)}), bf16[128,64,128]{2,1,0:T(8,128)(2,1)S(1)}, u32[]{:S(2)}, u32[]{:S(2)}) async-start(bf16[128,64,128]{2,1,0:T(8,128)(2,1)} %copy-done.2), calls=%async_computation | async-start | bytes 4194304 | tf_op jit(solution)/shard_map/all_to_all | solution.py:215
  32.8 0.0 copy-done.14
  32.8 0.1 reshape.9.queries
  32.9 0.0 copy-done.9
  32.9 0.0 copy-done.11
  33.0 0.0 copy-done.12
  33.0 0.0 copy-start
  33.0 2.2 %copy-done = bf16[4,256,2048]{2,1,0:T(8,128)(2,1)S(1)} copy-done((bf16[4,256,2048]{2,1,0:T(8,128)(2,1)S(1)}, bf16[4,256,2048]{2,1,0:T(8,128)(2,1)}, u32[]{:S(2)}) %copy-start) | copy-done | bytes 4194328
  35.2 0.0 copy-start.13
  35.2 8.4 %resident.1 = (bf16[4,8,64,128]{3,2,1,0:T(8,128)(2,1)S(1)}, f32[4,8,64,128]{3,2,1,0:T(8,128)S(1)}, f32[4,8,64,128]{3,2,1,0:T(8,128)S(1)}, f32[4,8,64,128]{3,2,1,0:T(8,128)S(1)}) custom-call(s32[32]{0:T(128)S(1)} %copy-done.11, f32[32,1024]{1,0:T(8,128)S(1)} %copy-done.9, bf16[16,16384]{1,0:T(8,128)(2,1)S(1)} %reshape.9.queries, ...), custom_call_target="tpu_custom_call" | custom-call | flops 268435456 | bytes 8521856 | tf_op jit(solution)/shard_map/resident/pallas_call | solution.py:188
  43.6 0.0 copy-start.3
  43.6 1.0 %copy-done.3 = f32[4,8,64,128]{3,2,1,0:T(8,128)} copy-done((f32[4,8,64,128]{3,2,1,0:T(8,128)}, f32[4,8,64,128]{3,2,1,0:T(8,128)S(1)}, u32[]{:S(2)}) %copy-start.3) | copy-done | bytes 1048600
  44.6 0.0 copy-start.5
  44.6 1.0 %copy-done.5 = f32[4,8,64,128]{3,2,1,0:T(8,128)} copy-done((f32[4,8,64,128]{3,2,1,0:T(8,128)}, f32[4,8,64,128]{3,2,1,0:T(8,128)S(1)}, u32[]{:S(2)}) %copy-start.5) | copy-done | bytes 1048600
  45.5 0.0 copy-start.7
  45.6 1.0 %copy-done.7 = f32[4,8,64,128]{3,2,1,0:T(8,128)} copy-done((f32[4,8,64,128]{3,2,1,0:T(8,128)}, f32[4,8,64,128]{3,2,1,0:T(8,128)S(1)}, u32[]{:S(2)}) %copy-start.7) | copy-done | bytes 1048600
  46.5 16.0 %all-to-all-done.arrived = bf16[128,64,128]{2,1,0:T(8,128)(2,1)S(1)} async-done(((bf16[128,64,128]{2,1,0:T(8,128)(2,1)}), bf16[128,64,128]{2,1,0:T(8,128)(2,1)S(1)}, u32[]{:S(2)}, u32[]{:S(2)}) %all-to-all-start) | async-done | bytes 2097184 | tf_op jit(solution)/shard_map/all_to_all | solution.py:215
  62.5 0.0 copy-done.13
  62.5 0.0 copy-start.4
  62.5 1.2 %copy-done.4 = f32[4,8,64,128]{3,2,1,0:T(8,128)S(1)} copy-done((f32[4,8,64,128]{3,2,1,0:T(8,128)S(1)}, f32[4,8,64,128]{3,2,1,0:T(8,128)}, u32[]{:S(2)}) %copy-start.4) | copy-done | bytes 1048600
  63.7 0.0 copy-start.6
  63.7 1.2 %copy-done.6 = f32[4,8,64,128]{3,2,1,0:T(8,128)S(1)} copy-done((f32[4,8,64,128]{3,2,1,0:T(8,128)S(1)}, f32[4,8,64,128]{3,2,1,0:T(8,128)}, u32[]{:S(2)}) %copy-start.6) | copy-done | bytes 1048600
  65.0 0.0 copy-start.8
  65.0 1.2 %copy-done.8 = f32[4,8,64,128]{3,2,1,0:T(8,128)S(1)} copy-done((f32[4,8,64,128]{3,2,1,0:T(8,128)S(1)}, f32[4,8,64,128]{3,2,1,0:T(8,128)}, u32[]{:S(2)}) %copy-start.8) | copy-done | bytes 1048600
  66.2 11.5 %arrived.1 = (bf16[4,128,2048]{2,1,0:T(8,128)(2,1)}, bf16[4,128]{1,0:T(4,128)(2,1)}, bf16[16,144,128]{2,1,0:T(8,128)(2,1)S(1)}) custom-call(s32[32]{0:T(128)S(1)} %copy-done.11, s32[32]{0:T(128)S(1)} %copy-done.13, bf16[128,64,128]{2,1,0:T(8,128)(2,1)S(1)} %all-to-all-done.arrived, f32[128,1,128]{2,1,0:T(1,128)S(1)} %all_to_all.15.arrived_scale, ...), custom_call_target="tpu_custom_call" | custom-call | flops 134217728 | bytes 8520960 | tf_op jit(solution)/shard_map/arrived/pallas_call | solution.py:188
  77.7 15.5 %all_to_all.16.partial = bf16[16,144,128]{2,1,0:T(8,128)(2,1)S(1)} all-to-all(bf16[16,144,128]{2,1,0:T(8,128)(2,1)S(1)} %get-tuple-element.18), channel_id=1, replica_groups=mesh['grp'=8,'seq'=16] {'seq'}, dimensions={0} | all-to-all | bytes 1179648 | tf_op jit(solution)/shard_map/all_to_all | solution.py:238
  93.2 1.2 %merge.1 = bf16[4,4,1024]{2,1,0:T(4,128)(2,1)} custom-call(bf16[16,144,128]{2,1,0:T(8,128)(2,1)S(1)} %all_to_all.16.partial), custom_call_target="tpu_custom_call" | custom-call | flops 524288 | bytes 622592 | tf_op jit(solution)/shard_map/merge/pallas_call | solution.py:188
Async XLA Ops:
  1.4 1.6 %copy-start.1 = (bf16[32,16,2048]{2,1,0:T(8,128)(2,1)S(1)}, bf16[32,16,2048]{2,1,0:T(8,128)(2,1)}, u32[]{:S(2)}) copy-start(bf16[32,16,2048]{2,1,0:T(8,128)(2,1)} %kv.2) | copy-start | bytes 6291460
  3.0 0.7 copy-start.10
  6.2 1.3 %copy-start.2 = (bf16[128,64,128]{2,1,0:T(8,128)(2,1)}, bf16[128,64,128]{2,1,0:T(8,128)(2,1)S(1)}, u32[]{:S(2)}) copy-start(bf16[128,64,128]{2,1,0:T(8,128)(2,1)S(1)} %get-tuple-element.12) | copy-start | bytes 6291460
  28.0 4.8 %copy-start.14 = (bf16[4,4,16384]{2,1,0:T(4,128)(2,1)S(1)}, bf16[4,4,16384]{2,1,0:T(4,128)(2,1)}, u32[]{:S(2)}) copy-start(bf16[4,4,16384]{2,1,0:T(4,128)(2,1)} %param.13) | copy-start | bytes 1572868
  28.0 5.0 %copy-start.9 = (f32[32,1024]{1,0:T(8,128)S(1)}, f32[32,1024]{1,0:T(8,128)}, u32[]{:S(2)}) copy-start(f32[32,1024]{1,0:T(8,128)} %k_scale.1) | copy-start | bytes 393220
  28.0 5.0 %copy-start.11 = (s32[32]{0:T(128)S(1)}, s32[32]{0:T(128)}, u32[]{:S(2)}) copy-start(s32[32]{0:T(128)} %route.5) | copy-start | bytes 388
  28.0 5.0 %copy-start.12 = (bf16[4,256]{1,0:T(4,128)(2,1)S(1)}, bf16[4,256]{1,0:T(4,128)(2,1)}, u32[]{:S(2)}) copy-start(bf16[4,256]{1,0:T(4,128)(2,1)} %vscale.2) | copy-start | bytes 6148
  28.0 34.5 %all-to-all-start = ((bf16[128,64,128]{2,1,0:T(8,128)(2,1)}), bf16[128,64,128]{2,1,0:T(8,128)(2,1)S(1)}, u32[]{:S(2)}, u32[]{:S(2)}) async-start(bf16[128,64,128]{2,1,0:T(8,128)(2,1)} %copy-done.2), calls=%async_computation | async-start | bytes 4194304 | tf_op jit(solution)/shard_map/all_to_all | solution.py:215
  33.0 2.2 %copy-start = (bf16[4,256,2048]{2,1,0:T(8,128)(2,1)S(1)}, bf16[4,256,2048]{2,1,0:T(8,128)(2,1)}, u32[]{:S(2)}) copy-start(bf16[4,256,2048]{2,1,0:T(8,128)(2,1)} %kv.3) | copy-start | bytes 12582916
  35.2 27.3 %copy-start.13 = (s32[32]{0:T(128)S(1)}, s32[32]{0:T(128)}, u32[]{:S(2)}) copy-start(s32[32]{0:T(128)} %lengths.1) | copy-start | bytes 388
  43.6 1.0 %copy-start.3 = (f32[4,8,64,128]{3,2,1,0:T(8,128)}, f32[4,8,64,128]{3,2,1,0:T(8,128)S(1)}, u32[]{:S(2)}) copy-start(f32[4,8,64,128]{3,2,1,0:T(8,128)S(1)} %get-tuple-element.15.numer) | copy-start | bytes 3145732
  44.6 1.0 %copy-start.5 = (f32[4,8,64,128]{3,2,1,0:T(8,128)}, f32[4,8,64,128]{3,2,1,0:T(8,128)S(1)}, u32[]{:S(2)}) copy-start(f32[4,8,64,128]{3,2,1,0:T(8,128)S(1)} %get-tuple-element.16.top) | copy-start | bytes 3145732
  45.5 1.0 %copy-start.7 = (f32[4,8,64,128]{3,2,1,0:T(8,128)}, f32[4,8,64,128]{3,2,1,0:T(8,128)S(1)}, u32[]{:S(2)}) copy-start(f32[4,8,64,128]{3,2,1,0:T(8,128)S(1)} %get-tuple-element.17.total) | copy-start | bytes 3145732
  62.5 1.2 %copy-start.4 = (f32[4,8,64,128]{3,2,1,0:T(8,128)S(1)}, f32[4,8,64,128]{3,2,1,0:T(8,128)}, u32[]{:S(2)}) copy-start(f32[4,8,64,128]{3,2,1,0:T(8,128)} %copy-done.3) | copy-start | bytes 3145732
  63.7 1.2 %copy-start.6 = (f32[4,8,64,128]{3,2,1,0:T(8,128)S(1)}, f32[4,8,64,128]{3,2,1,0:T(8,128)}, u32[]{:S(2)}) copy-start(f32[4,8,64,128]{3,2,1,0:T(8,128)} %copy-done.5) | copy-start | bytes 3145732
  65.0 1.2 %copy-start.8 = (f32[4,8,64,128]{3,2,1,0:T(8,128)S(1)}, f32[4,8,64,128]{3,2,1,0:T(8,128)}, u32[]{:S(2)}) copy-start(f32[4,8,64,128]{3,2,1,0:T(8,128)} %copy-done.7) | copy-start | bytes 3145732

commit v2 on v1

v2 whole, which is shorter than its diff:
```python
import jax
import jax.numpy as jnp
from jax import lax
from jax.experimental import pallas as pl
from jax.experimental.pallas import tpu as pltpu
from jax.sharding import PartitionSpec as P

HEAD_DIM = 128
LANES = 128
DEAD = -1e30
MIB = 1 << 20
PACK_UNROLL = 2
RES_LIMIT = 16
ARR_LIMIT = 16
PACK_LIMIT = 60
BLOCK_UNROLL = 2
HEAD_UNROLL = 2


def swap_matrix():
    row = lax.broadcasted_iota(jnp.int32, (256, 256), 0)
    col = lax.broadcasted_iota(jnp.int32, (256, 256), 1)
    hit = (row // 16 == col % 16) & (row % 16 == col // 16)
    return jnp.where(hit, 1.0, 0.0).astype(jnp.bfloat16)


def pack_kernel(route_hbm, kv_hbm, vscale, out_hbm, mark, route, kv, out, scale, route_sem, in_sems, out_sems):
    requests = kv.shape[0]
    groups = requests // 4
    step = requests // 4
    copy_route = pltpu.make_async_copy(route_hbm, route, route_sem)
    copy_route.start()
    for c in range(4):
        part = pl.ds(c * step, step)
        pltpu.make_async_copy(kv_hbm.at[part], kv.at[part], in_sems.at[c]).start()
    swap = swap_matrix()
    mark[...] = jnp.zeros_like(mark)
    scale[...] = jnp.zeros_like(scale)
    scale[:, 0:requests] = vscale[...].astype(jnp.float32)
    row = lax.broadcasted_iota(jnp.int32, (16, 8, LANES), 1)
    lines = jnp.broadcast_to(scale[...][:, None, :], (16, 8, LANES))
    lines = jnp.where(row == lax.axis_index("seq") % 8, lines, 0.0).astype(jnp.bfloat16)
    for g in range(groups):
        out[g * 16 : (g + 1) * 16, 64:72, :] = lines
    copy_route.wait()
    for c in range(4):
        part = pl.ds(c * step, step)
        pltpu.make_async_copy(kv_hbm.at[part], kv.at[part], in_sems.at[c]).wait()

    def one_group(g, carry):
        chosen = [route[g * 4 + i] for i in range(4)]
        for pair in range(2):
            tiles = []
            for l4 in range(4):
                for i in range(4):
                    halves = [
                        kv[chosen[i], :, pl.ds((lg * 4 + l4) * LANES, LANES)]
                        for lg in (2 * pair, 2 * pair + 1)
                    ]
                    tiles.append(jnp.concatenate(halves, axis=1))
            moved = jnp.dot(
                swap, jnp.concatenate(tiles, axis=0), preferred_element_type=jnp.float32
            ).astype(jnp.bfloat16)
            for half in range(2):
                block = moved[:, half * LANES : (half + 1) * LANES].reshape(16, 16, LANES)
                out[pl.ds(g * 16, 16), pl.ds((2 * pair + half) * 16, 16), :] = block
        rows = pl.ds(g * 16, 16)
        pltpu.make_async_copy(out.at[rows], out_hbm.at[rows], out_sems.at[g]).start()
        return carry

    lax.fori_loop(0, groups, one_group, 0, unroll=PACK_UNROLL)
    for g in range(groups):
        rows = pl.ds(g * 16, 16)
        pltpu.make_async_copy(out.at[rows], out_hbm.at[rows], out_sems.at[g]).wait()


def resident_kernel(
    route, lengths, k_scale, queries, kv, vscale,
    query_cols, numer, level, mask, chosen_rows, chosen_cols,
    head_scale, scale_cols,
):
    group = lax.axis_index("grp")
    split = lax.axis_index("seq")
    request_row = lax.broadcasted_iota(jnp.int32, (LANES, LANES), 0)
    request_lane = lax.broadcasted_iota(jnp.int32, (16, LANES), 1)
    slot_row = lax.broadcasted_iota(jnp.int32, (16, LANES), 0)
    rows = jnp.zeros((16, LANES), jnp.float32)
    for j in range(4):
        request = route[group * 4 + j]
        mask[j] = jnp.where(request_row * 16 + split < lengths[request], 0.0, DEAD)
        chosen_cols[:, j * LANES : (j + 1) * LANES] = jnp.where(
            request_row == request, 1.0, 0.0
        ).astype(jnp.bfloat16)
        rows = jnp.where((slot_row == j) & (request_lane == request), 1.0, rows)
    chosen_rows[...] = rows.astype(jnp.bfloat16)
    out_row = lax.broadcasted_iota(jnp.int32, (256, 256), 0)
    in_row = lax.broadcasted_iota(jnp.int32, (256, 256), 1)
    head = (out_row // 32 % 2) * 8 + out_row % 8
    slot_step = out_row // 64 * 4 + out_row // 8 % 4
    hit = (in_row // 16 == head) & (in_row % 16 == slot_step)
    order = jnp.where(hit, 1.0, 0.0).astype(jnp.bfloat16)
    first = lax.broadcasted_iota(jnp.int32, (LANES, LANES), 1) < 64
    for j in range(4):
        row = k_scale[pl.ds(route[group * 4 + j], 1), :]
        for n in range(8):
            head_scale[j * 8 + n : j * 8 + n + 1, :] = row[:, n * LANES : (n + 1) * LANES]
        line = vscale[j : j + 1, :].astype(jnp.float32)
        scale_cols[j] = jnp.broadcast_to(line, (LANES, 256)).T

    def scale_pair(p, carry):
        ordered = []
        for n in range(2):
            tiles = [
                queries[:, pl.ds(pl.multiple_of((p * 32 + n * 16 + h) * LANES, LANES), LANES)]
                for h in range(16)
            ]
            ordered.append(
                jnp.dot(order, jnp.concatenate(tiles, axis=0), preferred_element_type=jnp.float32)
            )
        for j in range(4):
            parts = [
                ordered[n][j * 64 : (j + 1) * 64]
                * head_scale[pl.ds(j * 8 + p * 2 + n, 1), :]
                * HEAD_DIM ** (-0.5)
                for n in range(2)
            ]
            cols = jnp.concatenate(parts, axis=0).T
            query_cols[j, p, 0:128] = jnp.where(first, cols, 0.0).astype(jnp.bfloat16)
            query_cols[j, p, 128:256] = jnp.where(first, 0.0, cols).astype(jnp.bfloat16)
        return carry

    lax.fori_loop(0, 4, scale_pair, 0)

    def one_pair(p, carry):
        lanes = pl.ds(pl.multiple_of(p * 256, 256), 256)
        value_lanes = pl.ds(pl.multiple_of(p * 256 + 1024, 256), 256)
        for j in range(4):
            scores = jnp.dot(kv[j, :, lanes], query_cols[j, p], preferred_element_type=jnp.float32)
            high = jnp.max(scores, axis=0, keepdims=True)
            expo = jnp.exp(scores - high)
            count = jnp.sum(expo, axis=0, keepdims=True)
            weight = (expo * scale_cols[j] * (1.0 / count)).T.astype(jnp.bfloat16)
            mixed = jnp.dot(weight, kv[j, :, value_lanes], preferred_element_type=jnp.float32)
            numer[j, p, 0:64] = mixed[0:64, 0:128].astype(jnp.bfloat16)
            numer[j, p, 64:128] = mixed[64:128, 128:256].astype(jnp.bfloat16)
            level[p, j : j + 1, :] = high + jnp.log(count)
        return carry

    lax.fori_loop(0, 4, one_pair, 0)


def arrived_kernel(
    arrived, query_cols, numer, level, mask, chosen_rows, chosen_cols,
    cache_hbm, cache_scale, partial,
    cache, stats, scale_cols, sems,
):
    swap = swap_matrix()

    def one_block(b, carry):
        tokens = pl.ds(pl.multiple_of(b * 16, 16), 16)
        for pair in range(2):
            halves = [
                arrived[tokens, pl.ds(lg * 16, 16), :].reshape(256, LANES)
                for lg in (2 * pair, 2 * pair + 1)
            ]
            moved = jnp.dot(
                swap, jnp.concatenate(halves, axis=1), preferred_element_type=jnp.float32
            ).astype(jnp.bfloat16)
            for half in range(2):
                for l4 in range(4):
                    for i in range(4):
                        at = (l4 * 4 + i) * 16
                        chunk = (2 * pair + half) * 4 + l4
                        cache[i, tokens, chunk * LANES : (chunk + 1) * LANES] = moved[
                            at : at + 16, half * LANES : (half + 1) * LANES
                        ]
        return carry

    lax.fori_loop(0, 8, one_block, 0, unroll=BLOCK_UNROLL)
    for j in range(4):
        pltpu.make_async_copy(cache.at[j], cache_hbm.at[j], sems.at[j]).start()
    scales = arrived[:, 64:72, :].astype(jnp.float32).reshape(16, 8, 8, LANES)
    scales = jnp.sum(scales, axis=1).reshape(LANES, LANES)
    for j in range(4):
        scale_cols[j] = jnp.dot(
            scales.astype(jnp.bfloat16),
            chosen_cols[:, j * LANES : (j + 1) * LANES],
            preferred_element_type=jnp.float32,
        )
    cache_scale[...] = jnp.dot(
        chosen_rows[...], scales.T.astype(jnp.bfloat16), preferred_element_type=jnp.float32
    )[0:4].astype(jnp.bfloat16)
    row = lax.broadcasted_iota(jnp.int32, (LANES, LANES), 0)
    diagonal = row == lax.broadcasted_iota(jnp.int32, (LANES, LANES), 1)
    stats[...] = jnp.zeros_like(stats)

    def one_pair(p, carry):
        lanes = pl.ds(pl.multiple_of(p * 256, 256), 256)
        value_lanes = pl.ds(pl.multiple_of(p * 256 + 1024, 256), 256)
        for j in range(4):
            scores = jnp.dot(cache[j, :, lanes], query_cols[j, p], preferred_element_type=jnp.float32)
            scores = scores + mask[j]
            before = level[p, j : j + 1, :]
            high = jnp.maximum(before, jnp.max(scores, axis=0, keepdims=True))
            high = high.astype(jnp.bfloat16).astype(jnp.float32)
            expo = jnp.exp(scores - high)
            keep = jnp.exp(before - high).astype(jnp.bfloat16).astype(jnp.float32)
            count = jnp.sum(expo, axis=0, keepdims=True) + keep
            coarse = count.astype(jnp.bfloat16).astype(jnp.float32)
            weight = (expo * scale_cols[j]).T.astype(jnp.bfloat16)
            held = jnp.where(diagonal, keep, 0.0).astype(jnp.bfloat16)
            old = numer[j, p]
            values = jnp.concatenate(
                [cache[j, :, value_lanes], jnp.concatenate([old, old], axis=1)], axis=0
            )
            mixed = jnp.dot(
                jnp.concatenate([weight, held], axis=1), values, preferred_element_type=jnp.float32
            ).astype(jnp.bfloat16)
            for c in range(4):
                part = slice(c // 2 * LANES, (c // 2 + 1) * LANES)
                partial[p * 4 + c, j * 32 : (j + 1) * 32, :] = mixed[c * 32 : (c + 1) * 32, part]
            stats[p, j : j + 1, :] = high
            stats[p, 4 + j : 5 + j, :] = coarse
            stats[p, 8 + j : 9 + j, :] = count - coarse
        return carry

    lax.fori_loop(0, 4, one_pair, 0, unroll=HEAD_UNROLL)
    for place in range(16):
        partial[place, 128:144, :] = stats[place // 4].astype(jnp.bfloat16)
    for j in range(4):
        pltpu.make_async_copy(cache.at[j], cache_hbm.at[j], sems.at[j]).wait()


def merge_kernel(partial, out, summed):
    splits = partial.shape[0]
    offset = lax.axis_index("seq") % 4
    stat = partial[:, 128:144, :].astype(jnp.float32)
    lane = lax.broadcasted_iota(jnp.int32, (splits, LANES), 1)
    share = jnp.zeros((splits, LANES), jnp.float32)
    for j in range(4):
        high = stat[:, j, :]
        count = stat[:, 4 + j, :] + stat[:, 8 + j, :]
        part = jnp.exp(high - jnp.max(high, axis=0, keepdims=True))
        part = part / jnp.sum(part * count, axis=0, keepdims=True)
        part = pltpu.roll(part, (j + 4 - offset) % 4 * 32, 1)
        share = jnp.where(lane // 32 == j, part, share)
    share = jnp.concatenate([share, jnp.zeros((LANES - splits, LANES), jnp.float32)], axis=0).T
    acc = partial[0, 0:128, :].astype(jnp.float32) * share[:, 0:1]
    for s in range(1, splits):
        acc = acc + partial[s, 0:128, :].astype(jnp.float32) * share[:, s : s + 1]
    summed[...] = acc
    for j in range(4):
        for h in range(8):
            out[j, :, h * HEAD_DIM : (h + 1) * HEAD_DIM] = summed[
                pl.ds(j * 32 + h, 4, stride=8), :
            ].astype(jnp.bfloat16)


def call(kernel, name, args, spaces, outs, out_spaces, scratch, limit, flops):
    moved = sum(a.size * a.dtype.itemsize for a in list(args) + list(outs))
    return pl.pallas_call(
        kernel,
        out_shape=outs,
        in_specs=[pl.BlockSpec(memory_space=s) for s in spaces],
        out_specs=[pl.BlockSpec(memory_space=s) for s in out_spaces],
        scratch_shapes=scratch,
        compiler_params=pltpu.CompilerParams(vmem_limit_bytes=limit * MIB),
        cost_estimate=pl.CostEstimate(flops=flops, bytes_accessed=moved, transcendentals=0),
        name=name,
    )(*args)


def body(
    prefill_kv, prefill_vscale, k_scale, resident_kv, resident_vscale, queries, route, lengths
):
    shape = jax.ShapeDtypeStruct
    bf16, f32 = jnp.bfloat16, jnp.float32
    smem, vmem, hbm = pltpu.SMEM, pltpu.VMEM, pltpu.HBM
    square = pltpu.VMEM((LANES, LANES), f32)
    dma = pltpu.SemaphoreType.DMA
    outgoing, mark = call(
        pack_kernel, "pack",
        (route, prefill_kv, prefill_vscale.T), (hbm, hbm, vmem),
        [shape((128, 72, LANES), bf16), shape((8, LANES), f32)], (hbm, vmem),
        [
            pltpu.SMEM((32,), jnp.int32), pltpu.VMEM((32, 16, 2048), bf16),
            pltpu.VMEM((128, 72, LANES), bf16), pltpu.VMEM((16, LANES), f32),
            dma, dma((4,)), dma((8,)),
        ],
        PACK_LIMIT, 2 * 256 * 256 * 4096,
    )
    arrived = lax.all_to_all(outgoing, ("grp", "seq"), split_axis=0, concat_axis=0, tiled=True)
    queries, _ = lax.optimization_barrier((queries, mark))
    query_cols, numer, level, mask, chosen_rows, chosen_cols = call(
        resident_kernel, "resident",
        (route, lengths, k_scale, queries.reshape(16, -1), resident_kv, resident_vscale),
        (smem,) * 2 + (vmem,) * 4,
        [
            shape((4, 4, 256, LANES), bf16), shape((4, 4, LANES, LANES), bf16),
            shape((4, 8, LANES), f32), shape((4, LANES, LANES), f32),
            shape((16, LANES), bf16), shape((LANES, 4 * LANES), bf16),
        ],
        (vmem,) * 6,
        [pltpu.VMEM((32, LANES), f32), pltpu.VMEM((4, 256, LANES), f32)],
        RES_LIMIT, 4 * 2048 * 256 * 128,
    )
    cache, cache_scale, partial = call(
        arrived_kernel, "arrived",
        (arrived, query_cols, numer, level, mask, chosen_rows, chosen_cols), (vmem,) * 7,
        [shape((4, 128, 2048), bf16), shape((4, 128), bf16), shape((16, 144, LANES), bf16)],
        (hbm, vmem, vmem),
        [
            pltpu.VMEM((4, 128, 2048), bf16), pltpu.VMEM((4, 16, LANES), f32),
            pltpu.VMEM((4, LANES, LANES), f32), dma((4,)),
        ],
        ARR_LIMIT, 4 * 2048 * 128 * 128,
    )
    swapped = lax.all_to_all(partial, "seq", split_axis=0, concat_axis=0, tiled=True)
    (attended,) = call(
        merge_kernel, "merge",
        (swapped,), (vmem,),
        [shape((4, 4, 1024), bf16)], (vmem,),
        [square], 8, 16 * 2 * 128 * 128,
    )
    return (attended, cache[None], cache_scale[None])


def solution(mesh):
    in_specs = (
        P(None, ("grp", "seq"), None),
        P(None, ("grp", "seq")),
        P(),
        P("grp", "seq", None),
        P("grp", "seq"),
        P("grp", None, None),
        P(),
        P(),
    )
    out_specs = (P("grp", None, "seq"), P("seq", "grp", None, None), P("seq", "grp", None))
    return jax.shard_map(body, mesh=mesh, in_specs=in_specs, out_specs=out_specs, check_vma=False)
```

time: 94.8 us -> 73.7 us (0.78)
  blocking collectives: 35.9 us -> 15.6 us
  starting transfers between devices: 4.8 us -> 11.2 us
  Pallas kernels: 23.7 us -> 17.9 us
  local copies, waits for them, and re-layouts: 13.2 us -> 11 us
    all_to_all x1 -> x0, blocking collectives: 20.4 us -> none  [body(): lax.all_to_all(out_scales, ('grp', 'seq'), split_axis=0, concat_axis=0, t...]
    all_to_all x1, starting transfers between devices: 4.8 us -> 11.2 us  [body(): lax.all_to_all(outgoing, ('grp', 'seq'), split_axis=0, concat_axis=0, til...]
    pallas_call x4, Pallas kernels: 23.7 us -> 17.9 us  [call(): pl.pallas_call(kernel, out_shape=outs, in_specs=[pl.BlockSpec(memory_spac...]
    unnamed x31 -> x28, local copies, waits for them, and re-layouts: 13.1 us -> 10.9 us
  transfers between devices with their start and end apart: 1 -> 1, of which waited for: 1 -> 1; matrix products, arithmetic and copies ran while one was open for 0% -> 0% of each run, Pallas kernels for 9% -> 11%
where the time goes in v2:
time: 73.7 us; the launch traced here: 73.3 us
  Pallas kernels  17.9 us (24%)
  waiting for transfers between devices  16.9 us (23%)
  blocking collectives  15.6 us (21%)
  starting transfers between devices  11.2 us (15%)
  local copies, waits for them, and re-layouts  11 us (15%)
    pallas_call x4, Pallas kernels, call(): pl.pallas_call(kernel, out_shape=outs, in_specs=[pl.BlockSpec(memory_spac...  17.9 us
    all_to_all x1, waiting for transfers between devices, body(): lax.all_to_all(outgoing, ('grp', 'seq'), split_axis=0, concat_axis=0, til...  16.9 us
    all_to_all x1, blocking collectives, body(): lax.all_to_all(partial, 'seq', split_axis=0, concat_axis=0, tiled=True)  15.6 us
    all_to_all x1, starting transfers between devices, body(): lax.all_to_all(outgoing, ('grp', 'seq'), split_axis=0, concat_axis=0, til...  11.2 us
    unnamed x28, local copies, waits for them, and re-layouts  10.9 us
  transfers between devices with their start and end apart: 1, of which 1 were waited for; matrix products, arithmetic and copies ran while one was open for 0% of the time, Pallas kernels for 11%

profile of v2, /device:TPU:0, one launch (start us, length us, event | category | flops | bytes accessed | tf_op | source)
XLA Modules:
  0.0 73.3 jit_solution(2210933091357363470)
XLA Ops:
  0.6 4.9 %pack.1 = (bf16[128,72,128]{2,1,0:T(8,128)(2,1)}, f32[8,128]{1,0:T(8,128)}) custom-call(s32[32]{0:T(128)} %route.1, bf16[32,16,2048]{2,1,0:T(8,128)(2,1)} %kv_hbm.1, bf16[16,32]{1,0:T(8,128)(2,1)} %bitcast.3), custom_call_target="tpu_custom_call" | custom-call | flops 536870912 | bytes 4461696 | tf_op jit(solution)/shard_map/pack/pallas_call | solution.py:261
  5.5 0.0 copy-start.13
  5.6 0.0 copy-start.5
  5.6 11.2 %all-to-all-start = ((bf16[128,72,128]{2,1,0:T(8,128)(2,1)}), bf16[128,72,128]{2,1,0:T(8,128)(2,1)S(1)}, u32[]{:S(2)}, u32[]{:S(2)}) async-start(bf16[128,72,128]{2,1,0:T(8,128)(2,1)} %get-tuple-element.13), calls=%async_computation | async-start | bytes 4718592 | tf_op jit(solution)/shard_map/all_to_all | solution.py:292
  16.7 0.0 copy-done.13
  16.7 0.1 reshape.9.queries
  16.9 0.0 copy-done.5
  16.9 0.0 copy-start
  16.9 2.2 %copy-done = bf16[4,256,2048]{2,1,0:T(8,128)(2,1)S(1)} copy-done((bf16[4,256,2048]{2,1,0:T(8,128)(2,1)S(1)}, bf16[4,256,2048]{2,1,0:T(8,128)(2,1)}, u32[]{:S(2)}) %copy-start) | copy-done | bytes 4194328
  19.1 0.0 copy-start.10
  19.1 0.7 copy-done.10
  19.7 0.0 copy-start.11
  19.8 0.7 copy-done.11
  20.4 0.0 copy-start.12
  20.4 0.7 copy-done.12
  21.1 8.3 %resident.1 = (bf16[4,4,256,128]{3,2,1,0:T(8,128)(2,1)S(1)}, bf16[4,4,128,128]{3,2,1,0:T(8,128)(2,1)S(1)}, f32[4,8,128]{2,1,0:T(8,128)S(1)}, f32[4,128,128]{2,1,...) custom-call(s32[32]{0:T(128)S(1)} %copy-done.11, s32[32]{0:T(128)S(1)} %copy-done.12, ...), custom_call_target="tpu_custom_call" | custom-call | flops 268435456 | bytes 6838528 | tf_op jit(solution)/shard_map/resident/pallas_call | solution.py:261
  29.4 0.0 copy-start.1
  29.4 1.0 %copy-done.1 = bf16[4,4,256,128]{3,2,1,0:T(8,128)(2,1)} copy-done((bf16[4,4,256,128]{3,2,1,0:T(8,128)(2,1)}, bf16[4,4,256,128]{3,2,1,0:T(8,128)(2,1)S(1)}, u32[]{:S(2)}) %copy-start.1) | copy-done | bytes 1048600
  30.4 0.0 copy-start.3
  30.4 0.7 copy-done.3
  31.1 0.0 copy-start.6
  31.1 0.6 copy-done.6
  31.7 0.0 copy-start.8
  31.7 0.6 copy-done.8
  32.3 16.9 %all-to-all-done.arrived = bf16[128,72,128]{2,1,0:T(8,128)(2,1)S(1)} async-done(((bf16[128,72,128]{2,1,0:T(8,128)(2,1)}), bf16[128,72,128]{2,1,0:T(8,128)(2,1)S(1)}, u32[]{:S(2)}, u32[]{:S(2)}) %all-to-all-start) | async-done | bytes 2359328 | tf_op jit(solution)/shard_map/all_to_all | solution.py:292
  49.2 0.0 copy-start.2
  49.2 1.2 %copy-done.2 = bf16[4,4,256,128]{3,2,1,0:T(8,128)(2,1)S(1)} copy-done((bf16[4,4,256,128]{3,2,1,0:T(8,128)(2,1)S(1)}, bf16[4,4,256,128]{3,2,1,0:T(8,128)(2,1)}, u32[]{:S(2)}) %copy-start.2) | copy-done | bytes 1048600
  50.4 0.0 copy-start.4
  50.4 0.9 %copy-done.4 = f32[4,128,128]{2,1,0:T(8,128)S(1)} copy-done((f32[4,128,128]{2,1,0:T(8,128)S(1)}, f32[4,128,128]{2,1,0:T(8,128)}, u32[]{:S(2)}) %copy-start.4) | copy-done | bytes 262168
  51.4 0.0 copy-start.7
  51.4 0.9 %copy-done.7 = bf16[128,512]{1,0:T(8,128)(2,1)S(1)} copy-done((bf16[128,512]{1,0:T(8,128)(2,1)S(1)}, bf16[128,512]{1,0:T(8,128)(2,1)}, u32[]{:S(2)}) %copy-start.7) | copy-done | bytes 131096
  52.3 0.0 copy-start.9
  52.3 0.7 copy-done.9
  53.0 3.4 %arrived.1 = (bf16[4,128,2048]{2,1,0:T(8,128)(2,1)}, bf16[4,128]{1,0:T(4,128)(2,1)}, bf16[16,144,128]{2,1,0:T(8,128)(2,1)S(1)}) custom-call(bf16[128,72,128]{2,1,0:T(8,128)(2,1)S(1)} %all-to-all-done.arrived, bf16[4,4,256,128]{3,2,1,0:T(8,128)(2,1)S(1)} %copy-done.2, bf16[4,4,128,128]{3,2,1,0:T(8,128)(2,1)S(1)} %get-tuple-element.15.numer, ...), custom_call_target="tpu_custom_call" | custom-call | flops 134217728 | bytes 7033856 | tf_op jit(solution)/shard_map/arrived/pallas_call | solution.py:261
  56.4 15.6 %all_to_all.10.partial = bf16[16,144,128]{2,1,0:T(8,128)(2,1)S(1)} all-to-all(bf16[16,144,128]{2,1,0:T(8,128)(2,1)S(1)} %get-tuple-element.20), channel_id=1, replica_groups=mesh['grp'=8,'seq'=16] {'seq'}, dimensions={0} | all-to-all | bytes 1179648 | tf_op jit(solution)/shard_map/all_to_all | solution.py:318
  72.0 1.3 %merge.1 = bf16[4,4,1024]{2,1,0:T(4,128)(2,1)} custom-call(bf16[16,144,128]{2,1,0:T(8,128)(2,1)S(1)} %all_to_all.10.partial), custom_call_target="tpu_custom_call" | custom-call | flops 524288 | bytes 622592 | tf_op jit(solution)/shard_map/merge/pallas_call | solution.py:261
Async XLA Ops:
  5.5 11.2 %copy-start.13 = (bf16[4,4,16384]{2,1,0:T(4,128)(2,1)S(1)}, bf16[4,4,16384]{2,1,0:T(4,128)(2,1)}, u32[]{:S(2)}) copy-start(bf16[4,4,16384]{2,1,0:T(4,128)(2,1)} %param.13) | copy-start | bytes 1572868
  5.6 11.3 %copy-start.5 = (f32[32,1024]{1,0:T(8,128)S(1)}, f32[32,1024]{1,0:T(8,128)}, u32[]{:S(2)}) copy-start(f32[32,1024]{1,0:T(8,128)} %k_scale.1) | copy-start | bytes 393220
  5.6 43.6 %all-to-all-start = ((bf16[128,72,128]{2,1,0:T(8,128)(2,1)}), bf16[128,72,128]{2,1,0:T(8,128)(2,1)S(1)}, u32[]{:S(2)}, u32[]{:S(2)}) async-start(bf16[128,72,128]{2,1,0:T(8,128)(2,1)} %get-tuple-element.13), calls=%async_computation | async-start | bytes 4718592 | tf_op jit(solution)/shard_map/all_to_all | solution.py:292
  16.9 2.2 %copy-start = (bf16[4,256,2048]{2,1,0:T(8,128)(2,1)S(1)}, bf16[4,256,2048]{2,1,0:T(8,128)(2,1)}, u32[]{:S(2)}) copy-start(bf16[4,256,2048]{2,1,0:T(8,128)(2,1)} %kv.1) | copy-start | bytes 12582916
  19.1 0.7 copy-start.10
  19.7 0.7 copy-start.11
  20.4 0.7 copy-start.12
  29.4 1.0 %copy-start.1 = (bf16[4,4,256,128]{3,2,1,0:T(8,128)(2,1)}, bf16[4,4,256,128]{3,2,1,0:T(8,128)(2,1)S(1)}, u32[]{:S(2)}) copy-start(bf16[4,4,256,128]{3,2,1,0:T(8,128)(2,1)S(1)} %get-tuple-element.14.query_cols) | copy-start | bytes 3145732
  30.4 0.7 copy-start.3
  31.1 0.6 copy-start.6
  31.7 0.6 copy-start.8
  49.2 1.2 %copy-start.2 = (bf16[4,4,256,128]{3,2,1,0:T(8,128)(2,1)S(1)}, bf16[4,4,256,128]{3,2,1,0:T(8,128)(2,1)}, u32[]{:S(2)}) copy-start(bf16[4,4,256,128]{3,2,1,0:T(8,128)(2,1)} %copy-done.1) | copy-start | bytes 3145732
  50.4 0.9 %copy-start.4 = (f32[4,128,128]{2,1,0:T(8,128)S(1)}, f32[4,128,128]{2,1,0:T(8,128)}, u32[]{:S(2)}) copy-start(f32[4,128,128]{2,1,0:T(8,128)} %copy-done.3) | copy-start | bytes 786436
  51.4 0.9 %copy-start.7 = (bf16[128,512]{1,0:T(8,128)(2,1)S(1)}, bf16[128,512]{1,0:T(8,128)(2,1)}, u32[]{:S(2)}) copy-start(bf16[128,512]{1,0:T(8,128)(2,1)} %copy-done.6) | copy-start | bytes 393220
  52.3 0.7 copy-start.9

commit v3 on v2

v3 whole, which is shorter than its diff:
```python
import math

import jax
import jax.numpy as jnp
from jax import lax
from jax.experimental import pallas as pl
from jax.experimental.pallas import tpu as pltpu
from jax.sharding import PartitionSpec as P

HEAD_DIM = 128
LANES = 128
DEAD = -1e30
MIB = 1 << 20
PACK_UNROLL = 8
RES_LIMIT = 16
ARR_LIMIT = 16
PACK_LIMIT = 16
BLOCK_UNROLL = 4
HEAD_UNROLL = 4


def two_heads(cols, first):
    none = jnp.zeros_like(cols)
    return jnp.concatenate([jnp.where(first, cols, none), jnp.where(first, none, cols)], axis=0)


def pack_kernel(
    route_hbm, kv_hbm, vscale_hbm, out_hbm, route, kv, vscale, out, scale, route_sem, scale_sem, in_sems, out_sems
):
    requests = kv.shape[0]
    groups = requests // 4
    step = requests // 4
    copy_route = pltpu.make_async_copy(route_hbm, route, route_sem)
    copy_route.start()
    copy_scale = pltpu.make_async_copy(vscale_hbm, vscale, scale_sem)
    copy_scale.start()
    for c in range(4):
        part = pl.ds(c * step, step)
        pltpu.make_async_copy(kv_hbm.at[part], kv.at[part], in_sems.at[c]).start()
    scale[...] = jnp.zeros_like(scale)
    copy_scale.wait()
    scale[:, 0:requests] = vscale[...].astype(jnp.float32)
    row = lax.broadcasted_iota(jnp.int32, (16, 4, LANES), 1)
    lines = jnp.broadcast_to(scale[...][:, None, :], (16, 4, LANES))
    lines = jnp.where(row == lax.axis_index("seq") % 4, lines, 0.0).astype(jnp.bfloat16)
    for g in range(groups):
        out[g * 16 : (g + 1) * 16, 16] = lines
    copy_route.wait()
    for c in range(4):
        part = pl.ds(c * step, step)
        pltpu.make_async_copy(kv_hbm.at[part], kv.at[part], in_sems.at[c]).wait()

    def one_group(g, carry):
        chosen = [route[g * 4 + i] for i in range(4)]
        for lg in range(4):
            tiles = [
                kv[chosen[i], :, pl.ds((lg * 4 + l4) * LANES, LANES)]
                for l4 in range(4)
                for i in range(4)
            ]
            block = jnp.swapaxes(jnp.stack(tiles, axis=0), 0, 1)
            out[pl.ds(g * 16, 16), lg * 4 : (lg + 1) * 4] = block.reshape(16, 4, 4, LANES)
        rows = pl.ds(g * 16, 16)
        pltpu.make_async_copy(out.at[rows], out_hbm.at[rows], out_sems.at[g]).start()
        return carry

    lax.fori_loop(0, groups, one_group, 0, unroll=PACK_UNROLL)
    for g in range(groups):
        rows = pl.ds(g * 16, 16)
        pltpu.make_async_copy(out.at[rows], out_hbm.at[rows], out_sems.at[g]).wait()


def resident_kernel(
    route, lengths, k_scale, queries, kv, vscale,
    held, level,
    head_scale, scale_cols, query_cols,
):
    group = lax.axis_index("grp")
    split = lax.axis_index("seq")
    for j in range(4):
        request = route[group * 4 + j]
        level[0, 4 + j : 5 + j, :] = jnp.full((1, LANES), request.astype(jnp.float32))
        live = lengths[request] - split
        level[1, 4 + j : 5 + j, :] = jnp.full((1, LANES), live.astype(jnp.float32))
    out_row = lax.broadcasted_iota(jnp.int32, (256, 256), 0)
    in_row = lax.broadcasted_iota(jnp.int32, (256, 256), 1)
    head = (out_row // 32 % 2) * 8 + out_row % 8
    slot_step = out_row // 64 * 4 + out_row // 8 % 4
    hit = (in_row // 16 == head) & (in_row % 16 == slot_step)
    order = jnp.where(hit, 1.0, 0.0).astype(jnp.bfloat16)
    first = lax.broadcasted_iota(jnp.int32, (LANES, LANES), 1) < 64
    for j in range(4):
        row = k_scale[pl.ds(route[group * 4 + j], 1), :]
        for n in range(8):
            head_scale[j * 8 + n : j * 8 + n + 1, :] = row[:, n * LANES : (n + 1) * LANES]
        line = vscale[j : j + 1, :].astype(jnp.float32)
        scale_cols[j] = jnp.broadcast_to(line, (LANES, 256)).T

    def scale_pair(p, carry):
        ordered = []
        for n in range(2):
            tiles = [
                queries[:, pl.ds(pl.multiple_of((p * 32 + n * 16 + h) * LANES, LANES), LANES)]
                for h in range(16)
            ]
            ordered.append(
                jnp.dot(order, jnp.concatenate(tiles, axis=0), preferred_element_type=jnp.float32)
            )
        for j in range(4):
            parts = [
                ordered[n][j * 64 : (j + 1) * 64]
                * head_scale[pl.ds(j * 8 + p * 2 + n, 1), :]
                * HEAD_DIM ** (-0.5)
                for n in range(2)
            ]
            cols = jnp.concatenate(parts, axis=0).T
            held[j, p, 0:128] = cols.astype(jnp.bfloat16)
            query_cols[j, p] = two_heads(cols.astype(jnp.bfloat16), first)
        return carry

    lax.fori_loop(0, 4, scale_pair, 0)

    def one_pair(p, carry):
        lanes = pl.ds(pl.multiple_of(p * 256, 256), 256)
        value_lanes = pl.ds(pl.multiple_of(p * 256 + 1024, 256), 256)
        for j in range(4):
            scores = jnp.dot(kv[j, :, lanes], query_cols[j, p], preferred_element_type=jnp.float32)
            high = jnp.max(scores, axis=0, keepdims=True)
            expo = jnp.exp(scores - high)
            count = jnp.sum(expo, axis=0, keepdims=True)
            weight = (expo * scale_cols[j] * (1.0 / count)).T.astype(jnp.bfloat16)
            mixed = jnp.dot(weight, kv[j, :, value_lanes], preferred_element_type=jnp.float32)
            held[j, p, 128:192] = mixed[0:64, 0:128].astype(jnp.bfloat16)
            held[j, p, 192:256] = mixed[64:128, 128:256].astype(jnp.bfloat16)
            level[p, j : j + 1, :] = high + jnp.log(count)
        return carry

    lax.fori_loop(0, 4, one_pair, 0)


def arrived_kernel(
    arrived, held_hbm, level, cache_hbm, cache_scale, partial, held, cache, stats, scale_cols, held_sem, sems
):
    bring = pltpu.make_async_copy(held_hbm, held, held_sem)
    bring.start()

    def one_block(b, carry):
        tokens = pl.ds(pl.multiple_of(b * 16, 16), 16)
        for lg in range(4):
            block = jnp.swapaxes(arrived[tokens, lg * 4 : (lg + 1) * 4].reshape(16, 16, LANES), 0, 1)
            for l4 in range(4):
                lanes = slice((lg * 4 + l4) * LANES, (lg * 4 + l4 + 1) * LANES)
                for i in range(4):
                    cache[i, tokens, lanes] = block[l4 * 4 + i]
        pltpu.make_async_copy(cache.at[:, tokens], cache_hbm.at[:, tokens], sems.at[b]).start()
        return carry

    lax.fori_loop(0, 8, one_block, 0, unroll=BLOCK_UNROLL)
    scales = arrived[:, 16].astype(jnp.float32).reshape(32, 4, 4, LANES)
    scales = jnp.sum(scales, axis=1).reshape(LANES, LANES)
    row = lax.broadcasted_iota(jnp.int32, (LANES, LANES), 0)
    lane = lax.broadcasted_iota(jnp.int32, (LANES, LANES), 1)
    row_number = row.astype(jnp.float32)
    by_token = scales.astype(jnp.bfloat16)
    for j in range(4):
        served = jnp.where(row_number == level[0, 4 + j : 5 + j, :], 1.0, 0.0).astype(jnp.bfloat16)
        columns = jnp.dot(by_token, served, preferred_element_type=jnp.float32)
        scale_cols[j] = columns
        cache_scale[j : j + 1, :] = columns.T[0:1].astype(jnp.bfloat16)
    diagonal = row == lane
    first = lane < 64
    token = row_number * 16.0
    stats[...] = jnp.zeros_like(stats)
    bring.wait()

    def one_pair(p, carry):
        lanes = pl.ds(pl.multiple_of(p * 256, 256), 256)
        value_lanes = pl.ds(pl.multiple_of(p * 256 + 1024, 256), 256)
        for j in range(4):
            columns = two_heads(held[j, p, 0:128], first)
            scores = jnp.dot(cache[j, :, lanes], columns, preferred_element_type=jnp.float32)
            scores = jnp.where(token < level[1, 4 + j : 5 + j, :], scores, DEAD)
            before = level[p, j : j + 1, :]
            high = jnp.maximum(before, jnp.max(scores, axis=0, keepdims=True))
            high = high.astype(jnp.bfloat16).astype(jnp.float32)
            expo = jnp.exp(scores - high)
            keep = jnp.exp(before - high).astype(jnp.bfloat16).astype(jnp.float32)
            count = jnp.sum(expo, axis=0, keepdims=True) + keep
            coarse = count.astype(jnp.bfloat16).astype(jnp.float32)
            weight = (expo * scale_cols[j]).T.astype(jnp.bfloat16)
            kept = jnp.where(diagonal, keep, 0.0).astype(jnp.bfloat16)
            old = held[j, p, 128:256]
            values = jnp.concatenate(
                [cache[j, :, value_lanes], jnp.concatenate([old, old], axis=1)], axis=0
            )
            mixed = jnp.dot(
                jnp.concatenate([weight, kept], axis=1), values, preferred_element_type=jnp.float32
            ).astype(jnp.bfloat16)
            for c in range(4):
                part = slice(c // 2 * LANES, (c // 2 + 1) * LANES)
                partial[p * 4 + c, j * 32 : (j + 1) * 32, :] = mixed[c * 32 : (c + 1) * 32, part]
            stats[p, j : j + 1, :] = high
            stats[p, 4 + j : 5 + j, :] = coarse
            stats[p, 8 + j : 9 + j, :] = count - coarse
        return carry

    lax.fori_loop(0, 4, one_pair, 0, unroll=HEAD_UNROLL)
    for place in range(16):
        partial[place, 128:144, :] = stats[place // 4].astype(jnp.bfloat16)
    for b in range(8):
        tokens = pl.ds(b * 16, 16)
        pltpu.make_async_copy(cache.at[:, tokens], cache_hbm.at[:, tokens], sems.at[b]).wait()


def merge_kernel(partial, out, summed):
    splits = partial.shape[0]
    offset = lax.axis_index("seq") % 4
    stat = partial[:, 128:144, :].astype(jnp.float32)
    lane = lax.broadcasted_iota(jnp.int32, (splits, LANES), 1)
    share = jnp.zeros((splits, LANES), jnp.float32)
    for j in range(4):
        high = stat[:, j, :]
        count = stat[:, 4 + j, :] + stat[:, 8 + j, :]
        part = jnp.exp(high - jnp.max(high, axis=0, keepdims=True))
        part = part / jnp.sum(part * count, axis=0, keepdims=True)
        part = pltpu.roll(part, (j + 4 - offset) % 4 * 32, 1)
        share = jnp.where(lane // 32 == j, part, share)
    share = jnp.concatenate([share, jnp.zeros((LANES - splits, LANES), jnp.float32)], axis=0).T
    acc = partial[0, 0:128, :].astype(jnp.float32) * share[:, 0:1]
    for s in range(1, splits):
        acc = acc + partial[s, 0:128, :].astype(jnp.float32) * share[:, s : s + 1]
    summed[...] = acc
    for j in range(4):
        for h in range(8):
            out[j, :, h * HEAD_DIM : (h + 1) * HEAD_DIM] = summed[
                pl.ds(j * 32 + h, 4, stride=8), :
            ].astype(jnp.bfloat16)


def call(kernel, name, args, spaces, outs, out_spaces, scratch, limit, flops):
    moved = sum(math.prod(a.shape) * a.dtype.itemsize for a in list(args) + list(outs))
    return pl.pallas_call(
        kernel,
        out_shape=outs,
        in_specs=[pl.BlockSpec(memory_space=s) for s in spaces],
        out_specs=[pl.BlockSpec(memory_space=s) for s in out_spaces],
        scratch_shapes=scratch,
        compiler_params=pltpu.CompilerParams(vmem_limit_bytes=limit * MIB),
        cost_estimate=pl.CostEstimate(flops=flops, bytes_accessed=moved, transcendentals=0),
        name=name,
    )(*args)


def hbm_of(x):
    return pltpu.with_memory_space_constraint(x, pltpu.HBM)


def body(
    prefill_kv, prefill_vscale, k_scale, resident_kv, resident_vscale, queries, route, lengths
):
    shape = jax.ShapeDtypeStruct
    bf16, f32 = jnp.bfloat16, jnp.float32
    smem, vmem, hbm = pltpu.SMEM, pltpu.VMEM, pltpu.HBM
    square = pltpu.VMEM((LANES, LANES), f32)
    dma = pltpu.SemaphoreType.DMA
    (outgoing,) = call(
        pack_kernel, "pack",
        (hbm_of(route), hbm_of(prefill_kv), hbm_of(prefill_vscale.T)), (hbm,) * 3,
        [hbm((128, 17, 4, LANES), bf16)], (hbm,),
        [
            pltpu.SMEM((32,), jnp.int32), pltpu.VMEM((32, 16, 2048), bf16),
            pltpu.VMEM((16, 32), bf16), pltpu.VMEM((128, 17, 4, LANES), bf16), pltpu.VMEM((16, LANES), f32),
            dma, dma, dma((4,)), dma((8,)),
        ],
        PACK_LIMIT, 2 * 256 * 256 * 4096,
    )
    arrived = lax.all_to_all(outgoing, ("grp", "seq"), split_axis=0, concat_axis=0, tiled=True)
    queries, _ = lax.optimization_barrier((queries, outgoing))
    held, level = call(
        resident_kernel, "resident",
        (route, lengths, k_scale, queries.reshape(16, -1), resident_kv, resident_vscale),
        (smem,) * 2 + (vmem,) * 4,
        [shape((4, 4, 256, LANES), bf16), shape((4, 8, LANES), f32)], (vmem,) * 2,
        [
            pltpu.VMEM((32, LANES), f32), pltpu.VMEM((4, 256, LANES), f32),
            pltpu.VMEM((4, 4, 256, LANES), bf16),
        ],
        RES_LIMIT, 4 * 2048 * 256 * 128,
    )
    cache, cache_scale, partial = call(
        arrived_kernel, "arrived",
        (arrived, hbm_of(held), level), (vmem, hbm, vmem),
        [shape((4, 128, 2048), bf16), shape((4, 128), bf16), shape((16, 144, LANES), bf16)],
        (hbm, vmem, vmem),
        [
            pltpu.VMEM((4, 4, 256, LANES), bf16), pltpu.VMEM((4, 128, 2048), bf16),
            pltpu.VMEM((4, 16, LANES), f32), pltpu.VMEM((4, LANES, LANES), f32), dma, dma((8,)),
        ],
        ARR_LIMIT, 4 * 2048 * 128 * 128,
    )
    swapped = lax.all_to_all(partial, "seq", split_axis=0, concat_axis=0, tiled=True)
    (attended,) = call(
        merge_kernel, "merge",
        (swapped,), (vmem,),
        [shape((4, 4, 1024), bf16)], (vmem,),
        [square], 8, 16 * 2 * 128 * 128,
    )
    return (attended, cache[None], cache_scale[None])


def solution(mesh):
    in_specs = (
        P(None, ("grp", "seq"), None),
        P(None, ("grp", "seq")),
        P(),
        P("grp", "seq", None),
        P("grp", "seq"),
        P("grp", None, None),
        P(),
        P(),
    )
    out_specs = (P("grp", None, "seq"), P("seq", "grp", None, None), P("seq", "grp", None))
    return jax.shard_map(body, mesh=mesh, in_specs=in_specs, out_specs=out_specs, check_vma=False)
```

time: 73.7 us -> 66.6 us (0.904)
  local copies, waits for them, and re-layouts: 11 us -> 3.3 us
  waiting for transfers between devices: 16.9 us -> 19.5 us
  Pallas kernels: 17.9 us -> 16.1 us
    unnamed x28 -> x14, local copies, waits for them, and re-layouts: 10.9 us -> 3.18 us
    all_to_all x1, waiting for transfers between devices: 16.9 us -> 19.5 us  [body(): lax.all_to_all(outgoing, ('grp', 'seq'), split_axis=0, concat_axis=0, til...]
    pallas_call x4, Pallas kernels: 17.9 us -> 16.1 us  [call(): pl.pallas_call(kernel, out_shape=outs, in_specs=[pl.BlockSpec(memory_spac...]
  transfers between devices with their start and end apart: 1 -> 1, of which waited for: 1 -> 1; matrix products, arithmetic and copies ran while one was open for 0% -> 0% of each run, Pallas kernels for 11% -> 12%
where the time goes in v3:
time: 66.6 us; the launch traced here: 66.3 us
  waiting for transfers between devices  19.5 us (29%)
  Pallas kernels  16.1 us (24%)
  blocking collectives  15.6 us (23%)
  starting transfers between devices  11.1 us (17%)
  local copies, waits for them, and re-layouts  3.3 us (5%)
  between operations  0.77 us (1%)
    all_to_all x1, waiting for transfers between devices, body(): lax.all_to_all(outgoing, ('grp', 'seq'), split_axis=0, concat_axis=0, til...  19.5 us
    pallas_call x4, Pallas kernels, call(): pl.pallas_call(kernel, out_shape=outs, in_specs=[pl.BlockSpec(memory_spac...  16.1 us
    all_to_all x1, blocking collectives, body(): lax.all_to_all(partial, 'seq', split_axis=0, concat_axis=0, tiled=True)  15.6 us
    all_to_all x1, starting transfers between devices, body(): lax.all_to_all(outgoing, ('grp', 'seq'), split_axis=0, concat_axis=0, til...  11.1 us
    unnamed x14, local copies, waits for them, and re-layouts  3.18 us
  transfers between devices with their start and end apart: 1, of which 1 were waited for; matrix products, arithmetic and copies ran while one was open for 0% of the time, Pallas kernels for 12%

profile of v3, /device:TPU:0, one launch (start us, length us, event | category | flops | bytes accessed | tf_op | source)
XLA Modules:
  0.0 66.3 jit_solution(517236674030569831)
XLA Ops:
  0.6 3.2 %pack.1 = bf16[128,17,4,128]{3,2,1,0:T(4,128)(2,1)} custom-call(s32[32]{0:T(128)} %route.1, bf16[32,16,2048]{2,1,0:T(8,128)(2,1)} %kv_hbm.1, bf16[16,32]{1,0:T(8,128)(2,1)} %bitcast.3), custom_call_target="tpu_custom_call" | custom-call | flops 536870912 | bytes 4326528 | tf_op jit(solution)/shard_map/pack/pallas_call | solution.py:242
  3.9 0.0 copy-start.6
  3.9 0.0 copy-start.2
  3.9 0.0 copy-start.3
  3.9 0.0 copy-start.4
  3.9 0.0 copy-start.5
  3.9 11.1 %all-to-all-start = ((bf16[128,17,4,128]{3,2,1,0:T(4,128)(2,1)}), bf16[128,17,4,128]{3,2,1,0:T(4,128)(2,1)S(1)}, u32[]{:S(2)}, u32[]{:S(2)}) async-start(bf16[128,17,4,128]{3,2,1,0:T(4,128)(2,1)} %pack.1), calls=%async_computation | async-start | bytes 4456448 | tf_op jit(solution)/shard_map/all_to_all | solution.py:277
  15.1 0.0 copy-done.6
  15.1 0.1 reshape.9.queries
  15.2 0.0 copy-done.2
  15.2 0.0 copy-done.3
  15.2 0.0 copy-done.4
  15.3 0.0 copy-done.5
  15.3 0.0 copy-start
  15.3 2.2 %copy-done = bf16[4,256,2048]{2,1,0:T(8,128)(2,1)S(1)} copy-done((bf16[4,256,2048]{2,1,0:T(8,128)(2,1)S(1)}, bf16[4,256,2048]{2,1,0:T(8,128)(2,1)}, u32[]{:S(2)}) %copy-start) | copy-done | bytes 4194328
  17.5 8.3 %resident.1 = (bf16[4,4,256,128]{3,2,1,0:T(8,128)(2,1)S(1)}, f32[4,8,128]{2,1,0:T(8,128)S(1)}) custom-call(s32[32]{0:T(128)S(1)} %copy-done.4, s32[32]{0:T(128)S(1)} %copy-done.5, f32[32,1024]{1,0:T(8,128)S(1)} %copy-done.2, bf16[16,16384]{1,0:T(8,128)(2,1)S(1)} %reshape.9.queries, bf16[4,256,2048]{2,1,0:T(8,128)(2,1)S(1)} %copy-done, ...), custom_call_target="tpu_custom_call" | custom-call | flops 268435456 | bytes 5916928 | tf_op jit(solution)/shard_map/resident/pallas_call | solution.py:242
  25.7 0.0 copy-start.1
  25.7 1.0 %copy-done.1 = bf16[4,4,256,128]{3,2,1,0:T(8,128)(2,1)} copy-done((bf16[4,4,256,128]{3,2,1,0:T(8,128)(2,1)}, bf16[4,4,256,128]{3,2,1,0:T(8,128)(2,1)S(1)}, u32[]{:S(2)}) %copy-start.1) | copy-done | bytes 1048600
  26.7 19.5 %all-to-all-done.arrived = bf16[128,17,4,128]{3,2,1,0:T(4,128)(2,1)S(1)} async-done(((bf16[128,17,4,128]{3,2,1,0:T(4,128)(2,1)}), bf16[128,17,4,128]{3,2,1,0:T(4,128)(2,1)S(1)}, u32[]{:S(2)}, u32[]{:S(2)}) %all-to-all-start) | async-done | bytes 2228256 | tf_op jit(solution)/shard_map/all_to_all | solution.py:277
  46.2 3.3 %arrived.1 = (bf16[4,128,2048]{2,1,0:T(8,128)(2,1)}, bf16[4,128]{1,0:T(4,128)(2,1)}, bf16[16,144,128]{2,1,0:T(8,128)(2,1)S(1)}) custom-call(bf16[128,17,4,128]{3,2,1,0:T(4,128)(2,1)S(1)} %all-to-all-done.arrived, bf16[4,4,256,128]{3,2,1,0:T(8,128)(2,1)} %copy-done.1, f32[4,8,128]{2,1,0:T(8,128)S(1)} %get-tuple-element.11.level), custom_call_target="tpu_custom_call" | custom-call | flops 134217728 | bytes 5981184 | tf_op jit(solution)/shard_map/arrived/pallas_call | solution.py:242
  49.5 15.6 %all_to_all.10.partial = bf16[16,144,128]{2,1,0:T(8,128)(2,1)S(1)} all-to-all(bf16[16,144,128]{2,1,0:T(8,128)(2,1)S(1)} %get-tuple-element.12), channel_id=1, replica_groups=mesh['grp'=8,'seq'=16] {'seq'}, dimensions={0} | all-to-all | bytes 1179648 | tf_op jit(solution)/shard_map/all_to_all | solution.py:301
  65.0 1.3 %merge.1 = bf16[4,4,1024]{2,1,0:T(4,128)(2,1)} custom-call(bf16[16,144,128]{2,1,0:T(8,128)(2,1)S(1)} %all_to_all.10.partial), custom_call_target="tpu_custom_call" | custom-call | flops 524288 | bytes 622592 | tf_op jit(solution)/shard_map/merge/pallas_call | solution.py:242
Async XLA Ops:
  3.9 11.2 %copy-start.6 = (bf16[4,4,16384]{2,1,0:T(4,128)(2,1)S(1)}, bf16[4,4,16384]{2,1,0:T(4,128)(2,1)}, u32[]{:S(2)}) copy-start(bf16[4,4,16384]{2,1,0:T(4,128)(2,1)} %param.13) | copy-start | bytes 1572868
  3.9 11.3 %copy-start.2 = (f32[32,1024]{1,0:T(8,128)S(1)}, f32[32,1024]{1,0:T(8,128)}, u32[]{:S(2)}) copy-start(f32[32,1024]{1,0:T(8,128)} %k_scale.1) | copy-start | bytes 393220
  3.9 11.3 %copy-start.3 = (bf16[4,256]{1,0:T(4,128)(2,1)S(1)}, bf16[4,256]{1,0:T(4,128)(2,1)}, u32[]{:S(2)}) copy-start(bf16[4,256]{1,0:T(4,128)(2,1)} %vscale.1) | copy-start | bytes 6148
  3.9 11.3 %copy-start.4 = (s32[32]{0:T(128)S(1)}, s32[32]{0:T(128)}, u32[]{:S(2)}) copy-start(s32[32]{0:T(128)} %route.1) | copy-start | bytes 388
  3.9 11.3 %copy-start.5 = (s32[32]{0:T(128)S(1)}, s32[32]{0:T(128)}, u32[]{:S(2)}) copy-start(s32[32]{0:T(128)} %lengths.1) | copy-start | bytes 388
  3.9 42.2 %all-to-all-start = ((bf16[128,17,4,128]{3,2,1,0:T(4,128)(2,1)}), bf16[128,17,4,128]{3,2,1,0:T(4,128)(2,1)S(1)}, u32[]{:S(2)}, u32[]{:S(2)}) async-start(bf16[128,17,4,128]{3,2,1,0:T(4,128)(2,1)} %pack.1), calls=%async_computation | async-start | bytes 4456448 | tf_op jit(solution)/shard_map/all_to_all | solution.py:277
  15.3 2.2 %copy-start = (bf16[4,256,2048]{2,1,0:T(8,128)(2,1)S(1)}, bf16[4,256,2048]{2,1,0:T(8,128)(2,1)}, u32[]{:S(2)}) copy-start(bf16[4,256,2048]{2,1,0:T(8,128)(2,1)} %kv.1) | copy-start | bytes 12582916
  25.7 1.0 %copy-start.1 = (bf16[4,4,256,128]{3,2,1,0:T(8,128)(2,1)}, bf16[4,4,256,128]{3,2,1,0:T(8,128)(2,1)S(1)}, u32[]{:S(2)}) copy-start(bf16[4,4,256,128]{3,2,1,0:T(8,128)(2,1)S(1)} %get-tuple-element.10.held_hbm) | copy-start | bytes 3145732

commit v4 on v3

--- a/solution.py
+++ b/solution.py
@@ -22,6 +22,11 @@
 def two_heads(cols, first):
     none = jnp.zeros_like(cols)
     return jnp.concatenate([jnp.where(first, cols, none), jnp.where(first, none, cols)], axis=0)
+
+
+def token_scales(arrived):
+    lines = arrived[:, 16].astype(jnp.float32).reshape(32, 4, 4, LANES)
+    return jnp.sum(lines, axis=1).reshape(LANES, LANES)
 
 
 def pack_kernel(
@@ -139,7 +144,7 @@
 
 
 def arrived_kernel(
-    arrived, held_hbm, level, cache_hbm, cache_scale, partial, held, cache, stats, scale_cols, held_sem, sems
+    arrived, held_hbm, level, partial, held, cache, stats, scale_cols, held_sem
 ):
     bring = pltpu.make_async_copy(held_hbm, held, held_sem)
     bring.start()
@@ -152,7 +157,6 @@
                 lanes = slice((lg * 4 + l4) * LANES, (lg * 4 + l4 + 1) * LANES)
                 for i in range(4):
                     cache[i, tokens, lanes] = block[l4 * 4 + i]
-        pltpu.make_async_copy(cache.at[:, tokens], cache_hbm.at[:, tokens], sems.at[b]).start()
         return carry
 
     lax.fori_loop(0, 8, one_block, 0, unroll=BLOCK_UNROLL)
@@ -164,9 +168,7 @@
     by_token = scales.astype(jnp.bfloat16)
     for j in range(4):
         served = jnp.where(row_number == level[0, 4 + j : 5 + j, :], 1.0, 0.0).astype(jnp.bfloat16)
-        columns = jnp.dot(by_token, served, preferred_element_type=jnp.float32)
-        scale_cols[j] = columns
-        cache_scale[j : j + 1, :] = columns.T[0:1].astype(jnp.bfloat16)
+        scale_cols[j] = jnp.dot(by_token, served, preferred_element_type=jnp.float32)
     diagonal = row == lane
     first = lane < 64
     token = row_number * 16.0
@@ -198,15 +200,42 @@
             ).astype(jnp.bfloat16)
             for c in range(4):
                 part = slice(c // 2 * LANES, (c // 2 + 1) * LANES)
-                partial[p * 4 + c, j * 32 : (j + 1) * 32, :] = mixed[c * 32 : (c + 1) * 32, part]
-            stats[p, j : j + 1, :] = high
-            stats[p, 4 + j : 5 + j, :] = coarse
-            stats[p, 8 + j : 9 + j, :] = count - coarse
+                partial[p * 4 + c, j * 8 : (j + 1) * 8] = mixed[c * 32 : (c + 1) * 32, part].reshape(8, 4, LANES)
+            stats[p, j, 0:1, :] = high
+            stats[p, j, 1:2, :] = coarse
+            stats[p, j, 2:3, :] = count - coarse
         return carry
 
     lax.fori_loop(0, 4, one_pair, 0, unroll=HEAD_UNROLL)
+    quarter = lax.broadcasted_iota(jnp.int32, (8, LANES), 1) // 32
     for place in range(16):
-        partial[place, 128:144, :] = stats[place // 4].astype(jnp.bfloat16)
+        lines = jnp.zeros((8, LANES), jnp.float32)
+        for j in range(4):
+            turned = stats[place // 4, j]
+            if j != place % 4:
+                turned = pltpu.roll(turned, (j - place) % 4 * 32, 1)
+            lines = jnp.where(quarter == j, turned, lines)
+        partial[place, 32] = lines[0:4].astype(jnp.bfloat16)
+
+
+def cache_kernel(arrived, level, cache_hbm, cache_scale, cache, sems):
+    def one_block(b, carry):
+        tokens = pl.ds(pl.multiple_of(b * 16, 16), 16)
+        for lg in range(4):
+            block = jnp.swapaxes(arrived[tokens, lg * 4 : (lg + 1) * 4].reshape(16, 16, LANES), 0, 1)
+            for l4 in range(4):
+                lanes = slice((lg * 4 + l4) * LANES, (lg * 4 + l4 + 1) * LANES)
+                for i in range(4):
+                    cache[i, tokens, lanes] = block[l4 * 4 + i]
+        pltpu.make_async_copy(cache.at[:, tokens], cache_hbm.at[:, tokens], sems.at[b]).start()
+        return carry
+
+    lax.fori_loop(0, 8, one_block, 0, unroll=2)
+    by_request = token_scales(arrived).T
+    row_number = lax.broadcasted_iota(jnp.int32, (LANES, LANES), 0).astype(jnp.float32)
+    for j in range(4):
+        served = jnp.where(row_number == level[0, 4 + j : 5 + j, :], by_request, 0.0)
+        cache_scale[j : j + 1, :] = jnp.sum(served, axis=0, keepdims=True).astype(jnp.bfloat16)
     for b in range(8):
         tokens = pl.ds(b * 16, 16)
         pltpu.make_async_copy(cache.at[:, tokens], cache_hbm.at[:, tokens], sems.at[b]).wait()
@@ -214,21 +243,16 @@
 
 def merge_kernel(partial, out, summed):
     splits = partial.shape[0]
-    offset = lax.axis_index("seq") % 4
-    stat = partial[:, 128:144, :].astype(jnp.float32)
-    lane = lax.broadcasted_iota(jnp.int32, (splits, LANES), 1)
-    share = jnp.zeros((splits, LANES), jnp.float32)
-    for j in range(4):
-        high = stat[:, j, :]
-        count = stat[:, 4 + j, :] + stat[:, 8 + j, :]
-        part = jnp.exp(high - jnp.max(high, axis=0, keepdims=True))
-        part = part / jnp.sum(part * count, axis=0, keepdims=True)
-        part = pltpu.roll(part, (j + 4 - offset) % 4 * 32, 1)
-        share = jnp.where(lane // 32 == j, part, share)
+    stat = partial[:, 32].astype(jnp.float32)
+    high = stat[:, 0, :]
+    count = stat[:, 1, :] + stat[:, 2, :]
+    share = jnp.exp(high - jnp.max(high, axis=0, keepdims=True))
+    share = share / jnp.sum(share * count, axis=0, keepdims=True)
     share = jnp.concatenate([share, jnp.zeros((LANES - splits, LANES), jnp.float32)], axis=0).T
-    acc = partial[0, 0:128, :].astype(jnp.float32) * share[:, 0:1]
+    acc = partial[0, 0:32].reshape(LANES, HEAD_DIM).astype(jnp.float32) * share[:, 0:1]
     for s in range(1, splits):
-        acc = acc + partial[s, 0:128, :].astype(jnp.float32) * share[:, s : s + 1]
+        rows = partial[s, 0:32].reshape(LANES, HEAD_DIM).astype(jnp.float32)
+        acc = acc + rows * share[:, s : s + 1]
     summed[...] = acc
     for j in range(4):
         for h in range(8):
@@ -287,16 +311,22 @@
         ],
         RES_LIMIT, 4 * 2048 * 256 * 128,
     )
-    cache, cache_scale, partial = call(
+    (partial,) = call(
         arrived_kernel, "arrived",
         (arrived, hbm_of(held), level), (vmem, hbm, vmem),
-        [shape((4, 128, 2048), bf16), shape((4, 128), bf16), shape((16, 144, LANES), bf16)],
-        (hbm, vmem, vmem),
+        [shape((16, 33, 4, LANES), bf16)], (vmem,),
         [
             pltpu.VMEM((4, 4, 256, LANES), bf16), pltpu.VMEM((4, 128, 2048), bf16),
-            pltpu.VMEM((4, 16, LANES), f32), pltpu.VMEM((4, LANES, LANES), f32), dma, dma((8,)),
+            pltpu.VMEM((4, 4, 8, LANES), f32), pltpu.VMEM((4, LANES, LANES), f32), dma,
         ],
         ARR_LIMIT, 4 * 2048 * 128 * 128,
+    )
+    cache, cache_scale = call(
+        cache_kernel, "cache",
+        (arrived, level), (vmem, vmem),
+        [hbm((4, 128, 2048), bf16), shape((4, 128), bf16)], (hbm, vmem),
+        [pltpu.VMEM((4, 128, 2048), bf16), dma((8,))],
+        ARR_LIMIT, 0,
     )
     swapped = lax.all_to_all(partial, "seq", split_axis=0, concat_axis=0, tiled=True)
     (attended,) = call(

time: 66.6 us -> 66 us (level)
  blocking collectives: 15.6 us -> 0 us
  waiting for transfers between devices: 19.5 us -> 28.4 us
  starting transfers between devices: 11.1 us -> 15.2 us
  Pallas kernels: 16.1 us -> 18 us
    all_to_all x1 -> x0, blocking collectives: 15.6 us -> none  [body(): lax.all_to_all(partial, 'seq', split_axis=0, concat_axis=0, tiled=True)]
    all_to_all x0 -> x1, waiting for transfers between devices: none -> 8.9 us  [body(): lax.all_to_all(partial, 'seq', split_axis=0, concat_axis=0, tiled=True)]
    all_to_all x0 -> x1, starting transfers between devices: none -> 4 us  [body(): lax.all_to_all(partial, 'seq', split_axis=0, concat_axis=0, tiled=True)]
    pallas_call x4 -> x5, Pallas kernels: 16.1 us -> 18 us  [call(): pl.pallas_call(kernel, out_shape=outs, in_specs=[pl.BlockSpec(memory_spac...]
  transfers between devices with their start and end apart: 1 -> 2, of which waited for: 1 -> 2; matrix products, arithmetic and copies ran while one was open for 0% -> 0% of each run, Pallas kernels for 12% -> 16%
where the time goes in v4:
time: 66 us; the launch traced here: 65.6 us
  waiting for transfers between devices  28.4 us (43%)
  Pallas kernels  18 us (27%)
  starting transfers between devices  15.2 us (23%)
  local copies, waits for them, and re-layouts  3.3 us (5%)
  between operations  0.78 us (1%)
    all_to_all x1, waiting for transfers between devices, body(): lax.all_to_all(outgoing, ('grp', 'seq'), split_axis=0, concat_axis=0, til...  19.5 us
    pallas_call x5, Pallas kernels, call(): pl.pallas_call(kernel, out_shape=outs, in_specs=[pl.BlockSpec(memory_spac...  18 us
    all_to_all x1, starting transfers between devices, body(): lax.all_to_all(outgoing, ('grp', 'seq'), split_axis=0, concat_axis=0, til...  11.1 us
    all_to_all x1, waiting for transfers between devices, body(): lax.all_to_all(partial, 'seq', split_axis=0, concat_axis=0, tiled=True)  8.9 us
    all_to_all x1, starting transfers between devices, body(): lax.all_to_all(partial, 'seq', split_axis=0, concat_axis=0, tiled=True)  4 us
    unnamed x14, local copies, waits for them, and re-layouts  3.18 us
  transfers between devices with their start and end apart: 2, of which 2 were waited for; matrix products, arithmetic and copies ran while one was open for 0% of the time, Pallas kernels for 16%

profile of v4, /device:TPU:0, one launch (start us, length us, event | category | flops | bytes accessed | tf_op | source)
XLA Modules:
  0.0 65.6 jit_solution(14007950472104194645)
XLA Ops:
  0.6 3.2 %pack.1 = bf16[128,17,4,128]{3,2,1,0:T(4,128)(2,1)} custom-call(s32[32]{0:T(128)} %route.1, bf16[32,16,2048]{2,1,0:T(8,128)(2,1)} %kv_hbm.1, bf16[16,32]{1,0:T(8,128)(2,1)} %bitcast.3), custom_call_target="tpu_custom_call" | custom-call | flops 536870912 | bytes 4326528 | tf_op jit(solution)/shard_map/pack/pallas_call | solution.py:266
  3.9 0.0 copy-start.6
  3.9 0.0 copy-start.2
  3.9 0.0 copy-start.3
  3.9 0.0 copy-start.4
  3.9 0.0 copy-start.5
  3.9 11.1 %all-to-all-start = ((bf16[128,17,4,128]{3,2,1,0:T(4,128)(2,1)}), bf16[128,17,4,128]{3,2,1,0:T(4,128)(2,1)S(1)}, u32[]{:S(2)}, u32[]{:S(2)}) async-start(bf16[128,17,4,128]{3,2,1,0:T(4,128)(2,1)} %pack.1), calls=%async_computation | async-start | bytes 4456448 | tf_op jit(solution)/shard_map/all_to_all | solution.py:301
  15.1 0.0 copy-done.6
  15.1 0.1 reshape.9.queries
  15.2 0.0 copy-done.2
  15.2 0.0 copy-done.3
  15.2 0.0 copy-done.4
  15.2 0.0 copy-done.5
  15.3 0.0 copy-start
  15.3 2.2 %copy-done = bf16[4,256,2048]{2,1,0:T(8,128)(2,1)S(1)} copy-done((bf16[4,256,2048]{2,1,0:T(8,128)(2,1)S(1)}, bf16[4,256,2048]{2,1,0:T(8,128)(2,1)}, u32[]{:S(2)}) %copy-start) | copy-done | bytes 4194328
  17.5 8.3 %resident.1 = (bf16[4,4,256,128]{3,2,1,0:T(8,128)(2,1)S(1)}, f32[4,8,128]{2,1,0:T(8,128)S(1)}) custom-call(s32[32]{0:T(128)S(1)} %copy-done.4, s32[32]{0:T(128)S(1)} %copy-done.5, f32[32,1024]{1,0:T(8,128)S(1)} %copy-done.2, bf16[16,16384]{1,0:T(8,128)(2,1)S(1)} %reshape.9.queries, bf16[4,256,2048]{2,1,0:T(8,128)(2,1)S(1)} %copy-done, ...), custom_call_target="tpu_custom_call" | custom-call | flops 268435456 | bytes 5916928 | tf_op jit(solution)/shard_map/resident/pallas_call | solution.py:266
  25.7 0.0 copy-start.1
  25.7 1.0 %copy-done.1 = bf16[4,4,256,128]{3,2,1,0:T(8,128)(2,1)} copy-done((bf16[4,4,256,128]{3,2,1,0:T(8,128)(2,1)}, bf16[4,4,256,128]{3,2,1,0:T(8,128)(2,1)S(1)}, u32[]{:S(2)}) %copy-start.1) | copy-done | bytes 1048600
  26.7 19.5 %all-to-all-done.arrived = bf16[128,17,4,128]{3,2,1,0:T(4,128)(2,1)S(1)} async-done(((bf16[128,17,4,128]{3,2,1,0:T(4,128)(2,1)}), bf16[128,17,4,128]{3,2,1,0:T(4,128)(2,1)S(1)}, u32[]{:S(2)}, u32[]{:S(2)}) %all-to-all-start) | async-done | bytes 2228256 | tf_op jit(solution)/shard_map/all_to_all | solution.py:301
  46.2 3.0 %arrived.1 = bf16[16,33,4,128]{3,2,1,0:T(4,128)(2,1)} custom-call(bf16[128,17,4,128]{3,2,1,0:T(4,128)(2,1)S(1)} %all-to-all-done.arrived, bf16[4,4,256,128]{3,2,1,0:T(8,128)(2,1)} %copy-done.1, f32[4,8,128]{2,1,0:T(8,128)S(1)} %get-tuple-element.10.level), custom_call_target="tpu_custom_call" | custom-call | flops 134217728 | bytes 3833856 | tf_op jit(solution)/shard_map/arrived/pallas_call | solution.py:266
  49.2 4.0 %all-to-all-start.1 = ((bf16[16,33,4,128]{3,2,1,0:T(4,128)(2,1)}), bf16[16,33,4,128]{3,2,1,0:T(4,128)(2,1)S(1)}, u32[]{:S(2)}, u32[]{:S(2)}) async-start(bf16[16,33,4,128]{3,2,1,0:T(4,128)(2,1)} %arrived.1), calls=%async_computation.1 | async-start | bytes 1081344 | tf_op jit(solution)/shard_map/all_to_all | solution.py:331
  53.2 2.3 %cache.1 = (bf16[4,128,2048]{2,1,0:T(8,128)(2,1)}, bf16[4,128]{1,0:T(4,128)(2,1)}) custom-call(bf16[128,17,4,128]{3,2,1,0:T(4,128)(2,1)S(1)} %all-to-all-done.arrived, f32[4,8,128]{2,1,0:T(8,128)S(1)} %get-tuple-element.10.level), custom_call_target="tpu_custom_call" | custom-call | bytes 4342784 | tf_op jit(solution)/shard_map/cache/pallas_call | solution.py:266
  55.5 8.9 %all-to-all-done.1.partial = bf16[16,33,4,128]{3,2,1,0:T(4,128)(2,1)S(1)} async-done(((bf16[16,33,4,128]{3,2,1,0:T(4,128)(2,1)}), bf16[16,33,4,128]{3,2,1,0:T(4,128)(2,1)S(1)}, u32[]{:S(2)}, u32[]{:S(2)}) %all-to-all-start.1) | async-done | bytes 540704 | tf_op jit(solution)/shard_map/all_to_all | solution.py:331
  64.4 1.2 %merge.1 = bf16[4,4,1024]{2,1,0:T(4,128)(2,1)} custom-call(bf16[16,33,4,128]{3,2,1,0:T(4,128)(2,1)S(1)} %all-to-all-done.1.partial), custom_call_target="tpu_custom_call" | custom-call | flops 524288 | bytes 573440 | tf_op jit(solution)/shard_map/merge/pallas_call | solution.py:266
Async XLA Ops:
  3.9 11.2 %copy-start.6 = (bf16[4,4,16384]{2,1,0:T(4,128)(2,1)S(1)}, bf16[4,4,16384]{2,1,0:T(4,128)(2,1)}, u32[]{:S(2)}) copy-start(bf16[4,4,16384]{2,1,0:T(4,128)(2,1)} %param.13) | copy-start | bytes 1572868
  3.9 11.3 %copy-start.2 = (f32[32,1024]{1,0:T(8,128)S(1)}, f32[32,1024]{1,0:T(8,128)}, u32[]{:S(2)}) copy-start(f32[32,1024]{1,0:T(8,128)} %k_scale.1) | copy-start | bytes 393220
  3.9 11.3 %copy-start.3 = (bf16[4,256]{1,0:T(4,128)(2,1)S(1)}, bf16[4,256]{1,0:T(4,128)(2,1)}, u32[]{:S(2)}) copy-start(bf16[4,256]{1,0:T(4,128)(2,1)} %vscale.1) | copy-start | bytes 6148
  3.9 11.3 %copy-start.4 = (s32[32]{0:T(128)S(1)}, s32[32]{0:T(128)}, u32[]{:S(2)}) copy-start(s32[32]{0:T(128)} %route.1) | copy-start | bytes 388
  3.9 11.3 %copy-start.5 = (s32[32]{0:T(128)S(1)}, s32[32]{0:T(128)}, u32[]{:S(2)}) copy-start(s32[32]{0:T(128)} %lengths.1) | copy-start | bytes 388
  3.9 42.2 %all-to-all-start = ((bf16[128,17,4,128]{3,2,1,0:T(4,128)(2,1)}), bf16[128,17,4,128]{3,2,1,0:T(4,128)(2,1)S(1)}, u32[]{:S(2)}, u32[]{:S(2)}) async-start(bf16[128,17,4,128]{3,2,1,0:T(4,128)(2,1)} %pack.1), calls=%async_computation | async-start | bytes 4456448 | tf_op jit(solution)/shard_map/all_to_all | solution.py:301
  15.3 2.2 %copy-start = (bf16[4,256,2048]{2,1,0:T(8,128)(2,1)S(1)}, bf16[4,256,2048]{2,1,0:T(8,128)(2,1)}, u32[]{:S(2)}) copy-start(bf16[4,256,2048]{2,1,0:T(8,128)(2,1)} %kv.1) | copy-start | bytes 12582916
  25.7 1.0 %copy-start.1 = (bf16[4,4,256,128]{3,2,1,0:T(8,128)(2,1)}, bf16[4,4,256,128]{3,2,1,0:T(8,128)(2,1)S(1)}, u32[]{:S(2)}) copy-start(bf16[4,4,256,128]{3,2,1,0:T(8,128)(2,1)S(1)} %get-tuple-element.9.held_hbm) | copy-start | bytes 3145732
  49.2 15.2 %all-to-all-start.1 = ((bf16[16,33,4,128]{3,2,1,0:T(4,128)(2,1)}), bf16[16,33,4,128]{3,2,1,0:T(4,128)(2,1)S(1)}, u32[]{:S(2)}, u32[]{:S(2)}) async-start(bf16[16,33,4,128]{3,2,1,0:T(4,128)(2,1)} %arrived.1), calls=%async_computation.1 | async-start | bytes 1081344 | tf_op jit(solution)/shard_map/all_to_all | solution.py:331

commit v5 on v4

--- a/solution.py
+++ b/solution.py
@@ -89,8 +89,8 @@
         level[1, 4 + j : 5 + j, :] = jnp.full((1, LANES), live.astype(jnp.float32))
     out_row = lax.broadcasted_iota(jnp.int32, (256, 256), 0)
     in_row = lax.broadcasted_iota(jnp.int32, (256, 256), 1)
-    head = (out_row // 32 % 2) * 8 + out_row % 8
-    slot_step = out_row // 64 * 4 + out_row // 8 % 4
+    head = (out_row // 32 % 2) * 8 + out_row // 4 % 8
+    slot_step = out_row // 64 * 4 + out_row % 4
     hit = (in_row // 16 == head) & (in_row % 16 == slot_step)
     order = jnp.where(hit, 1.0, 0.0).astype(jnp.bfloat16)
     first = lax.broadcasted_iota(jnp.int32, (LANES, LANES), 1) < 64
@@ -177,7 +177,9 @@
 
     def one_pair(p, carry):
         lanes = pl.ds(pl.multiple_of(p * 256, 256), 256)
-        value_lanes = pl.ds(pl.multiple_of(p * 256 + 1024, 256), 256)
+        value_lanes = [
+            pl.ds(pl.multiple_of(p * 256 + 1024 + n * LANES, LANES), LANES) for n in range(2)
+        ]
         for j in range(4):
             columns = two_heads(held[j, p, 0:128], first)
             scores = jnp.dot(cache[j, :, lanes], columns, preferred_element_type=jnp.float32)
@@ -192,15 +194,15 @@
             weight = (expo * scale_cols[j]).T.astype(jnp.bfloat16)
             kept = jnp.where(diagonal, keep, 0.0).astype(jnp.bfloat16)
             old = held[j, p, 128:256]
-            values = jnp.concatenate(
-                [cache[j, :, value_lanes], jnp.concatenate([old, old], axis=1)], axis=0
-            )
-            mixed = jnp.dot(
-                jnp.concatenate([weight, kept], axis=1), values, preferred_element_type=jnp.float32
-            ).astype(jnp.bfloat16)
-            for c in range(4):
-                part = slice(c // 2 * LANES, (c // 2 + 1) * LANES)
-                partial[p * 4 + c, j * 8 : (j + 1) * 8] = mixed[c * 32 : (c + 1) * 32, part].reshape(8, 4, LANES)
+            blend = jnp.concatenate([weight, kept], axis=1)
+            for n in range(2):
+                values = jnp.concatenate([cache[j, :, value_lanes[n]], old], axis=0)
+                mixed = jnp.dot(
+                    blend[n * 64 : (n + 1) * 64], values, preferred_element_type=jnp.float32
+                ).astype(jnp.bfloat16)
+                for c in range(2):
+                    part = mixed[c * 32 : (c + 1) * 32].reshape(8, 4, LANES)
+                    partial[p * 4 + n * 2 + c, j * 8 : (j + 1) * 8] = part
             stats[p, j, 0:1, :] = high
             stats[p, j, 1:2, :] = coarse
             stats[p, j, 2:3, :] = count - coarse
@@ -241,7 +243,7 @@
         pltpu.make_async_copy(cache.at[:, tokens], cache_hbm.at[:, tokens], sems.at[b]).wait()
 
 
-def merge_kernel(partial, out, summed):
+def merge_kernel(partial, out):
     splits = partial.shape[0]
     stat = partial[:, 32].astype(jnp.float32)
     high = stat[:, 0, :]
@@ -253,12 +255,10 @@
     for s in range(1, splits):
         rows = partial[s, 0:32].reshape(LANES, HEAD_DIM).astype(jnp.float32)
         acc = acc + rows * share[:, s : s + 1]
-    summed[...] = acc
     for j in range(4):
         for h in range(8):
-            out[j, :, h * HEAD_DIM : (h + 1) * HEAD_DIM] = summed[
-                pl.ds(j * 32 + h, 4, stride=8), :
-            ].astype(jnp.bfloat16)
+            rows = acc[j * 32 + h * 4 : j * 32 + (h + 1) * 4].astype(jnp.bfloat16)
+            out[j, :, h * HEAD_DIM : (h + 1) * HEAD_DIM] = rows
 
 
 def call(kernel, name, args, spaces, outs, out_spaces, scratch, limit, flops):
@@ -333,7 +333,7 @@
         merge_kernel, "merge",
         (swapped,), (vmem,),
         [shape((4, 4, 1024), bf16)], (vmem,),
-        [square], 8, 16 * 2 * 128 * 128,
+        [], 8, 16 * 2 * 128 * 128,
     )
     return (attended, cache[None], cache_scale[None])
 

time: 66 us -> 66 us (level)
  no operation moved by 1% of the time
where the time goes in v5:
time: 66 us; the launch traced here: 65.7 us
  waiting for transfers between devices  28.4 us (43%)
  Pallas kernels  18.1 us (27%)
  starting transfers between devices  15.2 us (23%)
  local copies, waits for them, and re-layouts  3.3 us (5%)
  between operations  0.78 us (1%)
    all_to_all x1, waiting for transfers between devices, body(): lax.all_to_all(outgoing, ('grp', 'seq'), split_axis=0, concat_axis=0, til...  19.5 us
    pallas_call x5, Pallas kernels, call(): pl.pallas_call(kernel, out_shape=outs, in_specs=[pl.BlockSpec(memory_spac...  18.1 us
    all_to_all x1, starting transfers between devices, body(): lax.all_to_all(outgoing, ('grp', 'seq'), split_axis=0, concat_axis=0, til...  11.1 us
    all_to_all x1, waiting for transfers between devices, body(): lax.all_to_all(partial, 'seq', split_axis=0, concat_axis=0, tiled=True)  8.9 us
    all_to_all x1, starting transfers between devices, body(): lax.all_to_all(partial, 'seq', split_axis=0, concat_axis=0, tiled=True)  4 us
    unnamed x14, local copies, waits for them, and re-layouts  3.18 us
  transfers between devices with their start and end apart: 2, of which 2 were waited for; matrix products, arithmetic and copies ran while one was open for 0% of the time, Pallas kernels for 16%

profile of v5, /device:TPU:0, one launch (start us, length us, event | category | flops | bytes accessed | tf_op | source)
XLA Modules:
  0.0 65.7 jit_solution(15306559550391001461)
XLA Ops:
  0.6 3.2 %pack.1 = bf16[128,17,4,128]{3,2,1,0:T(4,128)(2,1)} custom-call(s32[32]{0:T(128)} %route.1, bf16[32,16,2048]{2,1,0:T(8,128)(2,1)} %kv_hbm.1, bf16[16,32]{1,0:T(8,128)(2,1)} %bitcast.3), custom_call_target="tpu_custom_call" | custom-call | flops 536870912 | bytes 4326528 | tf_op jit(solution)/shard_map/pack/pallas_call | solution.py:266
  3.9 0.0 copy-start.6
  3.9 0.0 copy-start.2
  3.9 0.0 copy-start.3
  3.9 0.0 copy-start.4
  3.9 0.0 copy-start.5
  3.9 11.1 %all-to-all-start = ((bf16[128,17,4,128]{3,2,1,0:T(4,128)(2,1)}), bf16[128,17,4,128]{3,2,1,0:T(4,128)(2,1)S(1)}, u32[]{:S(2)}, u32[]{:S(2)}) async-start(bf16[128,17,4,128]{3,2,1,0:T(4,128)(2,1)} %pack.1), calls=%async_computation | async-start | bytes 4456448 | tf_op jit(solution)/shard_map/all_to_all | solution.py:301
  15.1 0.0 copy-done.6
  15.1 0.1 reshape.9.queries
  15.2 0.0 copy-done.2
  15.2 0.0 copy-done.3
  15.2 0.0 copy-done.4
  15.2 0.0 copy-done.5
  15.3 0.0 copy-start
  15.3 2.2 %copy-done = bf16[4,256,2048]{2,1,0:T(8,128)(2,1)S(1)} copy-done((bf16[4,256,2048]{2,1,0:T(8,128)(2,1)S(1)}, bf16[4,256,2048]{2,1,0:T(8,128)(2,1)}, u32[]{:S(2)}) %copy-start) | copy-done | bytes 4194328
  17.5 8.3 %resident.1 = (bf16[4,4,256,128]{3,2,1,0:T(8,128)(2,1)S(1)}, f32[4,8,128]{2,1,0:T(8,128)S(1)}) custom-call(s32[32]{0:T(128)S(1)} %copy-done.4, s32[32]{0:T(128)S(1)} %copy-done.5, f32[32,1024]{1,0:T(8,128)S(1)} %copy-done.2, bf16[16,16384]{1,0:T(8,128)(2,1)S(1)} %reshape.9.queries, bf16[4,256,2048]{2,1,0:T(8,128)(2,1)S(1)} %copy-done, ...), custom_call_target="tpu_custom_call" | custom-call | flops 268435456 | bytes 5916928 | tf_op jit(solution)/shard_map/resident/pallas_call | solution.py:266
  25.7 0.0 copy-start.1
  25.8 1.0 %copy-done.1 = bf16[4,4,256,128]{3,2,1,0:T(8,128)(2,1)} copy-done((bf16[4,4,256,128]{3,2,1,0:T(8,128)(2,1)}, bf16[4,4,256,128]{3,2,1,0:T(8,128)(2,1)S(1)}, u32[]{:S(2)}) %copy-start.1) | copy-done | bytes 1048600
  26.7 19.5 %all-to-all-done.arrived = bf16[128,17,4,128]{3,2,1,0:T(4,128)(2,1)S(1)} async-done(((bf16[128,17,4,128]{3,2,1,0:T(4,128)(2,1)}), bf16[128,17,4,128]{3,2,1,0:T(4,128)(2,1)S(1)}, u32[]{:S(2)}, u32[]{:S(2)}) %all-to-all-start) | async-done | bytes 2228256 | tf_op jit(solution)/shard_map/all_to_all | solution.py:301
  46.2 3.1 %arrived.1 = bf16[16,33,4,128]{3,2,1,0:T(4,128)(2,1)} custom-call(bf16[128,17,4,128]{3,2,1,0:T(4,128)(2,1)S(1)} %all-to-all-done.arrived, bf16[4,4,256,128]{3,2,1,0:T(8,128)(2,1)} %copy-done.1, f32[4,8,128]{2,1,0:T(8,128)S(1)} %get-tuple-element.10.level), custom_call_target="tpu_custom_call" | custom-call | flops 134217728 | bytes 3833856 | tf_op jit(solution)/shard_map/arrived/pallas_call | solution.py:266
  49.2 4.0 %all-to-all-start.1 = ((bf16[16,33,4,128]{3,2,1,0:T(4,128)(2,1)}), bf16[16,33,4,128]{3,2,1,0:T(4,128)(2,1)S(1)}, u32[]{:S(2)}, u32[]{:S(2)}) async-start(bf16[16,33,4,128]{3,2,1,0:T(4,128)(2,1)} %arrived.1), calls=%async_computation.1 | async-start | bytes 1081344 | tf_op jit(solution)/shard_map/all_to_all | solution.py:331
  53.2 2.3 %cache.1 = (bf16[4,128,2048]{2,1,0:T(8,128)(2,1)}, bf16[4,128]{1,0:T(4,128)(2,1)}) custom-call(bf16[128,17,4,128]{3,2,1,0:T(4,128)(2,1)S(1)} %all-to-all-done.arrived, f32[4,8,128]{2,1,0:T(8,128)S(1)} %get-tuple-element.10.level), custom_call_target="tpu_custom_call" | custom-call | bytes 4342784 | tf_op jit(solution)/shard_map/cache/pallas_call | solution.py:266
  55.6 8.9 %all-to-all-done.1.partial = bf16[16,33,4,128]{3,2,1,0:T(4,128)(2,1)S(1)} async-done(((bf16[16,33,4,128]{3,2,1,0:T(4,128)(2,1)}), bf16[16,33,4,128]{3,2,1,0:T(4,128)(2,1)S(1)}, u32[]{:S(2)}, u32[]{:S(2)}) %all-to-all-start.1) | async-done | bytes 540704 | tf_op jit(solution)/shard_map/all_to_all | solution.py:331
  64.5 1.2 %merge.1 = bf16[4,4,1024]{2,1,0:T(4,128)(2,1)} custom-call(bf16[16,33,4,128]{3,2,1,0:T(4,128)(2,1)S(1)} %all-to-all-done.1.partial), custom_call_target="tpu_custom_call" | custom-call | flops 524288 | bytes 573440 | tf_op jit(solution)/shard_map/merge/pallas_call | solution.py:266
Async XLA Ops:
  3.9 11.2 %copy-start.6 = (bf16[4,4,16384]{2,1,0:T(4,128)(2,1)S(1)}, bf16[4,4,16384]{2,1,0:T(4,128)(2,1)}, u32[]{:S(2)}) copy-start(bf16[4,4,16384]{2,1,0:T(4,128)(2,1)} %param.13) | copy-start | bytes 1572868
  3.9 11.3 %copy-start.2 = (f32[32,1024]{1,0:T(8,128)S(1)}, f32[32,1024]{1,0:T(8,128)}, u32[]{:S(2)}) copy-start(f32[32,1024]{1,0:T(8,128)} %k_scale.1) | copy-start | bytes 393220
  3.9 11.3 %copy-start.3 = (bf16[4,256]{1,0:T(4,128)(2,1)S(1)}, bf16[4,256]{1,0:T(4,128)(2,1)}, u32[]{:S(2)}) copy-start(bf16[4,256]{1,0:T(4,128)(2,1)} %vscale.1) | copy-start | bytes 6148
  3.9 11.3 %copy-start.4 = (s32[32]{0:T(128)S(1)}, s32[32]{0:T(128)}, u32[]{:S(2)}) copy-start(s32[32]{0:T(128)} %route.1) | copy-start | bytes 388
  3.9 11.3 %copy-start.5 = (s32[32]{0:T(128)S(1)}, s32[32]{0:T(128)}, u32[]{:S(2)}) copy-start(s32[32]{0:T(128)} %lengths.1) | copy-start | bytes 388
  3.9 42.2 %all-to-all-start = ((bf16[128,17,4,128]{3,2,1,0:T(4,128)(2,1)}), bf16[128,17,4,128]{3,2,1,0:T(4,128)(2,1)S(1)}, u32[]{:S(2)}, u32[]{:S(2)}) async-start(bf16[128,17,4,128]{3,2,1,0:T(4,128)(2,1)} %pack.1), calls=%async_computation | async-start | bytes 4456448 | tf_op jit(solution)/shard_map/all_to_all | solution.py:301
  15.3 2.2 %copy-start = (bf16[4,256,2048]{2,1,0:T(8,128)(2,1)S(1)}, bf16[4,256,2048]{2,1,0:T(8,128)(2,1)}, u32[]{:S(2)}) copy-start(bf16[4,256,2048]{2,1,0:T(8,128)(2,1)} %kv.1) | copy-start | bytes 12582916
  25.7 1.0 %copy-start.1 = (bf16[4,4,256,128]{3,2,1,0:T(8,128)(2,1)}, bf16[4,4,256,128]{3,2,1,0:T(8,128)(2,1)S(1)}, u32[]{:S(2)}) copy-start(bf16[4,4,256,128]{3,2,1,0:T(8,128)(2,1)S(1)} %get-tuple-element.9.held_hbm) | copy-start | bytes 3145732
  49.2 15.2 %all-to-all-start.1 = ((bf16[16,33,4,128]{3,2,1,0:T(4,128)(2,1)}), bf16[16,33,4,128]{3,2,1,0:T(4,128)(2,1)S(1)}, u32[]{:S(2)}, u32[]{:S(2)}) async-start(bf16[16,33,4,128]{3,2,1,0:T(4,128)(2,1)} %arrived.1), calls=%async_computation.1 | async-start | bytes 1081344 | tf_op jit(solution)/shard_map/all_to_all | solution.py:331

commit v6 on v5

--- a/solution.py
+++ b/solution.py
@@ -144,7 +144,7 @@
 
 
 def arrived_kernel(
-    arrived, held_hbm, level, partial, held, cache, stats, scale_cols, held_sem
+    arrived, held_hbm, level, cache_hbm, cache_scale, partial, held, cache, stats, scale_cols, held_sem, sems
 ):
     bring = pltpu.make_async_copy(held_hbm, held, held_sem)
     bring.start()
@@ -157,6 +157,7 @@
                 lanes = slice((lg * 4 + l4) * LANES, (lg * 4 + l4 + 1) * LANES)
                 for i in range(4):
                     cache[i, tokens, lanes] = block[l4 * 4 + i]
+        pltpu.make_async_copy(cache.at[:, tokens], cache_hbm.at[:, tokens], sems.at[b]).start()
         return carry
 
     lax.fori_loop(0, 8, one_block, 0, unroll=BLOCK_UNROLL)
@@ -168,7 +169,9 @@
     by_token = scales.astype(jnp.bfloat16)
     for j in range(4):
         served = jnp.where(row_number == level[0, 4 + j : 5 + j, :], 1.0, 0.0).astype(jnp.bfloat16)
-        scale_cols[j] = jnp.dot(by_token, served, preferred_element_type=jnp.float32)
+        columns = jnp.dot(by_token, served, preferred_element_type=jnp.float32)
+        scale_cols[j] = columns
+        cache_scale[j : j + 1, :] = columns.T[0:1].astype(jnp.bfloat16)
     diagonal = row == lane
     first = lane < 64
     token = row_number * 16.0
@@ -218,26 +221,6 @@
                 turned = pltpu.roll(turned, (j - place) % 4 * 32, 1)
             lines = jnp.where(quarter == j, turned, lines)
         partial[place, 32] = lines[0:4].astype(jnp.bfloat16)
-
-
-def cache_kernel(arrived, level, cache_hbm, cache_scale, cache, sems):
-    def one_block(b, carry):
-        tokens = pl.ds(pl.multiple_of(b * 16, 16), 16)
-        for lg in range(4):
-            block = jnp.swapaxes(arrived[tokens, lg * 4 : (lg + 1) * 4].reshape(16, 16, LANES), 0, 1)
-            for l4 in range(4):
-                lanes = slice((lg * 4 + l4) * LANES, (lg * 4 + l4 + 1) * LANES)
-                for i in range(4):
-                    cache[i, tokens, lanes] = block[l4 * 4 + i]
-        pltpu.make_async_copy(cache.at[:, tokens], cache_hbm.at[:, tokens], sems.at[b]).start()
-        return carry
-
-    lax.fori_loop(0, 8, one_block, 0, unroll=2)
-    by_request = token_scales(arrived).T
-    row_number = lax.broadcasted_iota(jnp.int32, (LANES, LANES), 0).astype(jnp.float32)
-    for j in range(4):
-        served = jnp.where(row_number == level[0, 4 + j : 5 + j, :], by_request, 0.0)
-        cache_scale[j : j + 1, :] = jnp.sum(served, axis=0, keepdims=True).astype(jnp.bfloat16)
     for b in range(8):
         tokens = pl.ds(b * 16, 16)
         pltpu.make_async_copy(cache.at[:, tokens], cache_hbm.at[:, tokens], sems.at[b]).wait()
@@ -311,22 +294,16 @@
         ],
         RES_LIMIT, 4 * 2048 * 256 * 128,
     )
-    (partial,) = call(
+    cache, cache_scale, partial = call(
         arrived_kernel, "arrived",
         (arrived, hbm_of(held), level), (vmem, hbm, vmem),
-        [shape((16, 33, 4, LANES), bf16)], (vmem,),
+        [hbm((4, 128, 2048), bf16), shape((4, 128), bf16), shape((16, 33, 4, LANES), bf16)],
+        (hbm, vmem, vmem),
         [
             pltpu.VMEM((4, 4, 256, LANES), bf16), pltpu.VMEM((4, 128, 2048), bf16),
-            pltpu.VMEM((4, 4, 8, LANES), f32), pltpu.VMEM((4, LANES, LANES), f32), dma,
+            pltpu.VMEM((4, 4, 8, LANES), f32), pltpu.VMEM((4, LANES, LANES), f32), dma, dma((8,)),
         ],
         ARR_LIMIT, 4 * 2048 * 128 * 128,
-    )
-    cache, cache_scale = call(
-        cache_kernel, "cache",
-        (arrived, level), (vmem, vmem),
-        [hbm((4, 128, 2048), bf16), shape((4, 128), bf16)], (hbm, vmem),
-        [pltpu.VMEM((4, 128, 2048), bf16), dma((8,))],
-        ARR_LIMIT, 0,
     )
     swapped = lax.all_to_all(partial, "seq", split_axis=0, concat_axis=0, tiled=True)
     (attended,) = call(

time: 66 us -> 66.3 us (level)
  blocking collectives: 0 us -> 15.2 us
  waiting for transfers between devices: 28.4 us -> 19.5 us
  starting transfers between devices: 15.2 us -> 11.1 us
  Pallas kernels: 18.1 us -> 16.1 us
    all_to_all x0 -> x1, blocking collectives: none -> 15.2 us  [body(): lax.all_to_all(partial, 'seq', split_axis=0, concat_axis=0, tiled=True)]
    all_to_all x1 -> x0, waiting for transfers between devices: 8.9 us -> none  [body(): lax.all_to_all(partial, 'seq', split_axis=0, concat_axis=0, tiled=True)]
    all_to_all x1 -> x0, starting transfers between devices: 4 us -> none  [body(): lax.all_to_all(partial, 'seq', split_axis=0, concat_axis=0, tiled=True)]
    pallas_call x5 -> x4, Pallas kernels: 18.1 us -> 16.1 us  [call(): pl.pallas_call(kernel, out_shape=outs, in_specs=[pl.BlockSpec(memory_spac...]
  transfers between devices with their start and end apart: 2 -> 1, of which waited for: 2 -> 1; matrix products, arithmetic and copies ran while one was open for 0% -> 0% of each run, Pallas kernels for 16% -> 13%
where the time goes in v6:
time: 66.3 us; the launch traced here: 66 us
  waiting for transfers between devices  19.5 us (29%)
  Pallas kernels  16.1 us (24%)
  blocking collectives  15.2 us (23%)
  starting transfers between devices  11.1 us (17%)
  local copies, waits for them, and re-layouts  3.3 us (5%)
  between operations  0.77 us (1%)
    all_to_all x1, waiting for transfers between devices, body(): lax.all_to_all(outgoing, ('grp', 'seq'), split_axis=0, concat_axis=0, til...  19.5 us
    pallas_call x4, Pallas kernels, call(): pl.pallas_call(kernel, out_shape=outs, in_specs=[pl.BlockSpec(memory_spac...  16.1 us
    all_to_all x1, blocking collectives, body(): lax.all_to_all(partial, 'seq', split_axis=0, concat_axis=0, tiled=True)  15.2 us
    all_to_all x1, starting transfers between devices, body(): lax.all_to_all(outgoing, ('grp', 'seq'), split_axis=0, concat_axis=0, til...  11.1 us
    unnamed x14, local copies, waits for them, and re-layouts  3.18 us
  transfers between devices with their start and end apart: 1, of which 1 were waited for; matrix products, arithmetic and copies ran while one was open for 0% of the time, Pallas kernels for 13%

profile of v6, /device:TPU:0, one launch (start us, length us, event | category | flops | bytes accessed | tf_op | source)
XLA Modules:
  0.0 66.0 jit_solution(477316082256546003)
XLA Ops:
  0.6 3.2 %pack.1 = bf16[128,17,4,128]{3,2,1,0:T(4,128)(2,1)} custom-call(s32[32]{0:T(128)} %route.1, bf16[32,16,2048]{2,1,0:T(8,128)(2,1)} %kv_hbm.1, bf16[16,32]{1,0:T(8,128)(2,1)} %bitcast.3), custom_call_target="tpu_custom_call" | custom-call | flops 536870912 | bytes 4326528 | tf_op jit(solution)/shard_map/pack/pallas_call | solution.py:249
  3.9 0.0 copy-start.6
  3.9 0.0 copy-start.2
  3.9 0.0 copy-start.3
  3.9 0.0 copy-start.4
  3.9 0.0 copy-start.5
  3.9 11.1 %all-to-all-start = ((bf16[128,17,4,128]{3,2,1,0:T(4,128)(2,1)}), bf16[128,17,4,128]{3,2,1,0:T(4,128)(2,1)S(1)}, u32[]{:S(2)}, u32[]{:S(2)}) async-start(bf16[128,17,4,128]{3,2,1,0:T(4,128)(2,1)} %pack.1), calls=%async_computation | async-start | bytes 4456448 | tf_op jit(solution)/shard_map/all_to_all | solution.py:284
  15.1 0.0 copy-done.6
  15.1 0.1 reshape.9.queries
  15.2 0.0 copy-done.2
  15.2 0.0 copy-done.3
  15.2 0.0 copy-done.4
  15.3 0.0 copy-done.5
  15.3 0.0 copy-start
  15.3 2.2 %copy-done = bf16[4,256,2048]{2,1,0:T(8,128)(2,1)S(1)} copy-done((bf16[4,256,2048]{2,1,0:T(8,128)(2,1)S(1)}, bf16[4,256,2048]{2,1,0:T(8,128)(2,1)}, u32[]{:S(2)}) %copy-start) | copy-done | bytes 4194328
  17.5 8.3 %resident.1 = (bf16[4,4,256,128]{3,2,1,0:T(8,128)(2,1)S(1)}, f32[4,8,128]{2,1,0:T(8,128)S(1)}) custom-call(s32[32]{0:T(128)S(1)} %copy-done.4, s32[32]{0:T(128)S(1)} %copy-done.5, f32[32,1024]{1,0:T(8,128)S(1)} %copy-done.2, bf16[16,16384]{1,0:T(8,128)(2,1)S(1)} %reshape.9.queries, bf16[4,256,2048]{2,1,0:T(8,128)(2,1)S(1)} %copy-done, ...), custom_call_target="tpu_custom_call" | custom-call | flops 268435456 | bytes 5916928 | tf_op jit(solution)/shard_map/resident/pallas_call | solution.py:249
  25.7 0.0 copy-start.1
  25.8 1.0 %copy-done.1 = bf16[4,4,256,128]{3,2,1,0:T(8,128)(2,1)} copy-done((bf16[4,4,256,128]{3,2,1,0:T(8,128)(2,1)}, bf16[4,4,256,128]{3,2,1,0:T(8,128)(2,1)S(1)}, u32[]{:S(2)}) %copy-start.1) | copy-done | bytes 1048600
  26.7 19.5 %all-to-all-done.arrived = bf16[128,17,4,128]{3,2,1,0:T(4,128)(2,1)S(1)} async-done(((bf16[128,17,4,128]{3,2,1,0:T(4,128)(2,1)}), bf16[128,17,4,128]{3,2,1,0:T(4,128)(2,1)S(1)}, u32[]{:S(2)}, u32[]{:S(2)}) %all-to-all-start) | async-done | bytes 2228256 | tf_op jit(solution)/shard_map/all_to_all | solution.py:284
  46.2 3.4 %arrived.1 = (bf16[4,128,2048]{2,1,0:T(8,128)(2,1)}, bf16[4,128]{1,0:T(4,128)(2,1)}, bf16[16,33,4,128]{3,2,1,0:T(4,128)(2,1)S(1)}) custom-call(bf16[128,17,4,128]{3,2,1,0:T(4,128)(2,1)S(1)} %all-to-all-done.arrived, bf16[4,4,256,128]{3,2,1,0:T(8,128)(2,1)} %copy-done.1, f32[4,8,128]{2,1,0:T(8,128)S(1)} %get-tuple-element.11.level), custom_call_target="tpu_custom_call" | custom-call | flops 134217728 | bytes 5932032 | tf_op jit(solution)/shard_map/arrived/pallas_call | solution.py:249
  49.5 15.2 %all_to_all.10.partial = bf16[16,33,4,128]{3,2,1,0:T(4,128)(2,1)S(1)} all-to-all(bf16[16,33,4,128]{3,2,1,0:T(4,128)(2,1)S(1)} %get-tuple-element.12), channel_id=1, replica_groups=mesh['grp'=8,'seq'=16] {'seq'}, dimensions={0} | all-to-all | bytes 1081344 | tf_op jit(solution)/shard_map/all_to_all | solution.py:308
  64.8 1.2 %merge.1 = bf16[4,4,1024]{2,1,0:T(4,128)(2,1)} custom-call(bf16[16,33,4,128]{3,2,1,0:T(4,128)(2,1)S(1)} %all_to_all.10.partial), custom_call_target="tpu_custom_call" | custom-call | flops 524288 | bytes 573440 | tf_op jit(solution)/shard_map/merge/pallas_call | solution.py:249
Async XLA Ops:
  3.9 11.2 %copy-start.6 = (bf16[4,4,16384]{2,1,0:T(4,128)(2,1)S(1)}, bf16[4,4,16384]{2,1,0:T(4,128)(2,1)}, u32[]{:S(2)}) copy-start(bf16[4,4,16384]{2,1,0:T(4,128)(2,1)} %param.13) | copy-start | bytes 1572868
  3.9 11.3 %copy-start.2 = (f32[32,1024]{1,0:T(8,128)S(1)}, f32[32,1024]{1,0:T(8,128)}, u32[]{:S(2)}) copy-start(f32[32,1024]{1,0:T(8,128)} %k_scale.1) | copy-start | bytes 393220
  3.9 11.3 %copy-start.3 = (bf16[4,256]{1,0:T(4,128)(2,1)S(1)}, bf16[4,256]{1,0:T(4,128)(2,1)}, u32[]{:S(2)}) copy-start(bf16[4,256]{1,0:T(4,128)(2,1)} %vscale.1) | copy-start | bytes 6148
  3.9 11.3 %copy-start.4 = (s32[32]{0:T(128)S(1)}, s32[32]{0:T(128)}, u32[]{:S(2)}) copy-start(s32[32]{0:T(128)} %route.1) | copy-start | bytes 388
  3.9 11.3 %copy-start.5 = (s32[32]{0:T(128)S(1)}, s32[32]{0:T(128)}, u32[]{:S(2)}) copy-start(s32[32]{0:T(128)} %lengths.1) | copy-start | bytes 388
  3.9 42.2 %all-to-all-start = ((bf16[128,17,4,128]{3,2,1,0:T(4,128)(2,1)}), bf16[128,17,4,128]{3,2,1,0:T(4,128)(2,1)S(1)}, u32[]{:S(2)}, u32[]{:S(2)}) async-start(bf16[128,17,4,128]{3,2,1,0:T(4,128)(2,1)} %pack.1), calls=%async_computation | async-start | bytes 4456448 | tf_op jit(solution)/shard_map/all_to_all | solution.py:284
  15.3 2.2 %copy-start = (bf16[4,256,2048]{2,1,0:T(8,128)(2,1)S(1)}, bf16[4,256,2048]{2,1,0:T(8,128)(2,1)}, u32[]{:S(2)}) copy-start(bf16[4,256,2048]{2,1,0:T(8,128)(2,1)} %kv.1) | copy-start | bytes 12582916
  25.7 1.0 %copy-start.1 = (bf16[4,4,256,128]{3,2,1,0:T(8,128)(2,1)}, bf16[4,4,256,128]{3,2,1,0:T(8,128)(2,1)S(1)}, u32[]{:S(2)}) copy-start(bf16[4,4,256,128]{3,2,1,0:T(8,128)(2,1)S(1)} %get-tuple-element.10.held_hbm) | copy-start | bytes 3145732

commit v7 on v5

--- a/solution.py
+++ b/solution.py
@@ -144,7 +144,7 @@
 
 
 def arrived_kernel(
-    arrived, held_hbm, level, partial, held, cache, stats, scale_cols, held_sem
+    arrived, held_hbm, level, partial_hbm, partial, held, cache, stats, scale_cols, held_sem, sems
 ):
     bring = pltpu.make_async_copy(held_hbm, held, held_sem)
     bring.start()
@@ -173,6 +173,7 @@
     first = lane < 64
     token = row_number * 16.0
     stats[...] = jnp.zeros_like(stats)
+    quarter = lax.broadcasted_iota(jnp.int32, (8, LANES), 1) // 32
     bring.wait()
 
     def one_pair(p, carry):
@@ -206,18 +207,22 @@
             stats[p, j, 0:1, :] = high
             stats[p, j, 1:2, :] = coarse
             stats[p, j, 2:3, :] = count - coarse
+        for c in range(4):
+            lines = jnp.zeros((8, LANES), jnp.float32)
+            for j in range(4):
+                turned = stats[p, j]
+                if j != c:
+                    turned = pltpu.roll(turned, (j - c) % 4 * 32, 1)
+                lines = jnp.where(quarter == j, turned, lines)
+            partial[p * 4 + c, 32] = lines[0:4].astype(jnp.bfloat16)
+        rows = pl.ds(p * 4, 4)
+        pltpu.make_async_copy(partial.at[rows], partial_hbm.at[rows], sems.at[p]).start()
         return carry
 
     lax.fori_loop(0, 4, one_pair, 0, unroll=HEAD_UNROLL)
-    quarter = lax.broadcasted_iota(jnp.int32, (8, LANES), 1) // 32
-    for place in range(16):
-        lines = jnp.zeros((8, LANES), jnp.float32)
-        for j in range(4):
-            turned = stats[place // 4, j]
-            if j != place % 4:
-                turned = pltpu.roll(turned, (j - place) % 4 * 32, 1)
-            lines = jnp.where(quarter == j, turned, lines)
-        partial[place, 32] = lines[0:4].astype(jnp.bfloat16)
+    for p in range(4):
+        rows = pl.ds(p * 4, 4)
+        pltpu.make_async_copy(partial.at[rows], partial_hbm.at[rows], sems.at[p]).wait()
 
 
 def cache_kernel(arrived, level, cache_hbm, cache_scale, cache, sems):
@@ -314,10 +319,11 @@
     (partial,) = call(
         arrived_kernel, "arrived",
         (arrived, hbm_of(held), level), (vmem, hbm, vmem),
-        [shape((16, 33, 4, LANES), bf16)], (vmem,),
+        [hbm((16, 33, 4, LANES), bf16)], (hbm,),
         [
+            pltpu.VMEM((16, 33, 4, LANES), bf16),
             pltpu.VMEM((4, 4, 256, LANES), bf16), pltpu.VMEM((4, 128, 2048), bf16),
-            pltpu.VMEM((4, 4, 8, LANES), f32), pltpu.VMEM((4, LANES, LANES), f32), dma,
+            pltpu.VMEM((4, 4, 8, LANES), f32), pltpu.VMEM((4, LANES, LANES), f32), dma, dma((4,)),
         ],
         ARR_LIMIT, 4 * 2048 * 128 * 128,
     )

time: 66 us -> 66 us (level)
  no operation moved by 1% of the time
where the time goes in v7:
time: 66 us; the launch traced here: 65.6 us
  waiting for transfers between devices  28.4 us (43%)
  Pallas kernels  18 us (27%)
  starting transfers between devices  15.2 us (23%)
  local copies, waits for them, and re-layouts  3.3 us (5%)
  between operations  0.78 us (1%)
    all_to_all x1, waiting for transfers between devices, body(): lax.all_to_all(outgoing, ('grp', 'seq'), split_axis=0, concat_axis=0, til...  19.5 us
    pallas_call x5, Pallas kernels, call(): pl.pallas_call(kernel, out_shape=outs, in_specs=[pl.BlockSpec(memory_spac...  18 us
    all_to_all x1, starting transfers between devices, body(): lax.all_to_all(outgoing, ('grp', 'seq'), split_axis=0, concat_axis=0, til...  11.1 us
    all_to_all x1, waiting for transfers between devices, body(): lax.all_to_all(partial, 'seq', split_axis=0, concat_axis=0, tiled=True)  8.9 us
    all_to_all x1, starting transfers between devices, body(): lax.all_to_all(partial, 'seq', split_axis=0, concat_axis=0, tiled=True)  4 us
    unnamed x14, local copies, waits for them, and re-layouts  3.18 us
  transfers between devices with their start and end apart: 2, of which 2 were waited for; matrix products, arithmetic and copies ran while one was open for 0% of the time, Pallas kernels for 16%

profile of v7, /device:TPU:0, one launch (start us, length us, event | category | flops | bytes accessed | tf_op | source)
XLA Modules:
  0.0 65.6 jit_solution(10834067484604810642)
XLA Ops:
  0.6 3.2 %pack.1 = bf16[128,17,4,128]{3,2,1,0:T(4,128)(2,1)} custom-call(s32[32]{0:T(128)} %route.1, bf16[32,16,2048]{2,1,0:T(8,128)(2,1)} %kv_hbm.1, bf16[16,32]{1,0:T(8,128)(2,1)} %bitcast.3), custom_call_target="tpu_custom_call" | custom-call | flops 536870912 | bytes 4326528 | tf_op jit(solution)/shard_map/pack/pallas_call | solution.py:271
  3.9 0.0 copy-start.6
  3.9 0.0 copy-start.2
  3.9 0.0 copy-start.3
  3.9 0.0 copy-start.4
  3.9 0.0 copy-start.5
  3.9 11.1 %all-to-all-start = ((bf16[128,17,4,128]{3,2,1,0:T(4,128)(2,1)}), bf16[128,17,4,128]{3,2,1,0:T(4,128)(2,1)S(1)}, u32[]{:S(2)}, u32[]{:S(2)}) async-start(bf16[128,17,4,128]{3,2,1,0:T(4,128)(2,1)} %pack.1), calls=%async_computation | async-start | bytes 4456448 | tf_op jit(solution)/shard_map/all_to_all | solution.py:306
  15.1 0.0 copy-done.6
  15.1 0.1 reshape.9.queries
  15.2 0.0 copy-done.2
  15.2 0.0 copy-done.3
  15.2 0.0 copy-done.4
  15.2 0.0 copy-done.5
  15.3 0.0 copy-start
  15.3 2.2 %copy-done = bf16[4,256,2048]{2,1,0:T(8,128)(2,1)S(1)} copy-done((bf16[4,256,2048]{2,1,0:T(8,128)(2,1)S(1)}, bf16[4,256,2048]{2,1,0:T(8,128)(2,1)}, u32[]{:S(2)}) %copy-start) | copy-done | bytes 4194328
  17.5 8.3 %resident.1 = (bf16[4,4,256,128]{3,2,1,0:T(8,128)(2,1)S(1)}, f32[4,8,128]{2,1,0:T(8,128)S(1)}) custom-call(s32[32]{0:T(128)S(1)} %copy-done.4, s32[32]{0:T(128)S(1)} %copy-done.5, f32[32,1024]{1,0:T(8,128)S(1)} %copy-done.2, bf16[16,16384]{1,0:T(8,128)(2,1)S(1)} %reshape.9.queries, bf16[4,256,2048]{2,1,0:T(8,128)(2,1)S(1)} %copy-done, ...), custom_call_target="tpu_custom_call" | custom-call | flops 268435456 | bytes 5916928 | tf_op jit(solution)/shard_map/resident/pallas_call | solution.py:271
  25.7 0.0 copy-start.1
  25.8 1.0 %copy-done.1 = bf16[4,4,256,128]{3,2,1,0:T(8,128)(2,1)} copy-done((bf16[4,4,256,128]{3,2,1,0:T(8,128)(2,1)}, bf16[4,4,256,128]{3,2,1,0:T(8,128)(2,1)S(1)}, u32[]{:S(2)}) %copy-start.1) | copy-done | bytes 1048600
  26.7 19.5 %all-to-all-done.arrived = bf16[128,17,4,128]{3,2,1,0:T(4,128)(2,1)S(1)} async-done(((bf16[128,17,4,128]{3,2,1,0:T(4,128)(2,1)}), bf16[128,17,4,128]{3,2,1,0:T(4,128)(2,1)S(1)}, u32[]{:S(2)}, u32[]{:S(2)}) %all-to-all-start) | async-done | bytes 2228256 | tf_op jit(solution)/shard_map/all_to_all | solution.py:306
  46.2 3.0 %arrived.1 = bf16[16,33,4,128]{3,2,1,0:T(4,128)(2,1)} custom-call(bf16[128,17,4,128]{3,2,1,0:T(4,128)(2,1)S(1)} %all-to-all-done.arrived, bf16[4,4,256,128]{3,2,1,0:T(8,128)(2,1)} %copy-done.1, f32[4,8,128]{2,1,0:T(8,128)S(1)} %get-tuple-element.10.level), custom_call_target="tpu_custom_call" | custom-call | flops 134217728 | bytes 3833856 | tf_op jit(solution)/shard_map/arrived/pallas_call | solution.py:271
  49.1 4.0 %all-to-all-start.1 = ((bf16[16,33,4,128]{3,2,1,0:T(4,128)(2,1)}), bf16[16,33,4,128]{3,2,1,0:T(4,128)(2,1)S(1)}, u32[]{:S(2)}, u32[]{:S(2)}) async-start(bf16[16,33,4,128]{3,2,1,0:T(4,128)(2,1)} %arrived.1), calls=%async_computation.1 | async-start | bytes 1081344 | tf_op jit(solution)/shard_map/all_to_all | solution.py:337
  53.2 2.3 %cache.1 = (bf16[4,128,2048]{2,1,0:T(8,128)(2,1)}, bf16[4,128]{1,0:T(4,128)(2,1)}) custom-call(bf16[128,17,4,128]{3,2,1,0:T(4,128)(2,1)S(1)} %all-to-all-done.arrived, f32[4,8,128]{2,1,0:T(8,128)S(1)} %get-tuple-element.10.level), custom_call_target="tpu_custom_call" | custom-call | bytes 4342784 | tf_op jit(solution)/shard_map/cache/pallas_call | solution.py:271
  55.5 8.9 %all-to-all-done.1.partial = bf16[16,33,4,128]{3,2,1,0:T(4,128)(2,1)S(1)} async-done(((bf16[16,33,4,128]{3,2,1,0:T(4,128)(2,1)}), bf16[16,33,4,128]{3,2,1,0:T(4,128)(2,1)S(1)}, u32[]{:S(2)}, u32[]{:S(2)}) %all-to-all-start.1) | async-done | bytes 540704 | tf_op jit(solution)/shard_map/all_to_all | solution.py:337
  64.4 1.2 %merge.1 = bf16[4,4,1024]{2,1,0:T(4,128)(2,1)} custom-call(bf16[16,33,4,128]{3,2,1,0:T(4,128)(2,1)S(1)} %all-to-all-done.1.partial), custom_call_target="tpu_custom_call" | custom-call | flops 524288 | bytes 573440 | tf_op jit(solution)/shard_map/merge/pallas_call | solution.py:271
Async XLA Ops:
  3.9 11.2 %copy-start.6 = (bf16[4,4,16384]{2,1,0:T(4,128)(2,1)S(1)}, bf16[4,4,16384]{2,1,0:T(4,128)(2,1)}, u32[]{:S(2)}) copy-start(bf16[4,4,16384]{2,1,0:T(4,128)(2,1)} %param.13) | copy-start | bytes 1572868
  3.9 11.3 %copy-start.2 = (f32[32,1024]{1,0:T(8,128)S(1)}, f32[32,1024]{1,0:T(8,128)}, u32[]{:S(2)}) copy-start(f32[32,1024]{1,0:T(8,128)} %k_scale.1) | copy-start | bytes 393220
  3.9 11.3 %copy-start.3 = (bf16[4,256]{1,0:T(4,128)(2,1)S(1)}, bf16[4,256]{1,0:T(4,128)(2,1)}, u32[]{:S(2)}) copy-start(bf16[4,256]{1,0:T(4,128)(2,1)} %vscale.1) | copy-start | bytes 6148
  3.9 11.3 %copy-start.4 = (s32[32]{0:T(128)S(1)}, s32[32]{0:T(128)}, u32[]{:S(2)}) copy-start(s32[32]{0:T(128)} %route.1) | copy-start | bytes 388
  3.9 11.3 %copy-start.5 = (s32[32]{0:T(128)S(1)}, s32[32]{0:T(128)}, u32[]{:S(2)}) copy-start(s32[32]{0:T(128)} %lengths.1) | copy-start | bytes 388
  3.9 42.2 %all-to-all-start = ((bf16[128,17,4,128]{3,2,1,0:T(4,128)(2,1)}), bf16[128,17,4,128]{3,2,1,0:T(4,128)(2,1)S(1)}, u32[]{:S(2)}, u32[]{:S(2)}) async-start(bf16[128,17,4,128]{3,2,1,0:T(4,128)(2,1)} %pack.1), calls=%async_computation | async-start | bytes 4456448 | tf_op jit(solution)/shard_map/all_to_all | solution.py:306
  15.3 2.2 %copy-start = (bf16[4,256,2048]{2,1,0:T(8,128)(2,1)S(1)}, bf16[4,256,2048]{2,1,0:T(8,128)(2,1)}, u32[]{:S(2)}) copy-start(bf16[4,256,2048]{2,1,0:T(8,128)(2,1)} %kv.1) | copy-start | bytes 12582916
  25.7 1.0 %copy-start.1 = (bf16[4,4,256,128]{3,2,1,0:T(8,128)(2,1)}, bf16[4,4,256,128]{3,2,1,0:T(8,128)(2,1)S(1)}, u32[]{:S(2)}) copy-start(bf16[4,4,256,128]{3,2,1,0:T(8,128)(2,1)S(1)} %get-tuple-element.9.held_hbm) | copy-start | bytes 3145732
  49.1 15.2 %all-to-all-start.1 = ((bf16[16,33,4,128]{3,2,1,0:T(4,128)(2,1)}), bf16[16,33,4,128]{3,2,1,0:T(4,128)(2,1)S(1)}, u32[]{:S(2)}, u32[]{:S(2)}) async-start(bf16[16,33,4,128]{3,2,1,0:T(4,128)(2,1)} %arrived.1), calls=%async_computation.1 | async-start | bytes 1081344 | tf_op jit(solution)/shard_map/all_to_all | solution.py:337
